TPU v7x, 512 devices: a whole 4x4x16 slice. The times are simulated.
512 devices in a mesh: replica: 32 (over z_lo, x), tp: 16 (over z_hi, y, core).
Axes of the slice: x: 4, y: 4, z: 16 (z_hi: 2, z_lo: 8; z = z_hi * 8 + z_lo), core: 2. Of those that a mesh axis runs over, the one named last changes fastest.
Arguments:
- kv_cache: bfloat16 [128, 2, 2048, 1024], P('replica', None, 'tp')
- lengths: int32 [128], P('replica'), may hold values from 2 to 2048, as said below
- queries: bfloat16 [3, 128, 64, 128], P(None, 'replica')
- new_kv: bfloat16 [3, 128, 2, 1024], P(None, 'replica'), may hold values from -6 to 6
- moving_slot: int32 [32], P('replica'), may hold values from 0 to 3
- destination: int32 [32], replicated, may hold values from 0 to 31, as said below
- block_index: int32 [32], P('replica'), may hold values from 0 to 3
Outputs:
- attended: bfloat16 [3, 128, 64, 128], P(None, 'replica', 'tp')
- arrived: bfloat16 [32, 2, 512, 1024], P('replica', None, 'tp')
- handed: bfloat16 [32, 3, 2, 1024], P('replica')
Inputs may be any that keep to these rules, and one draw needn't show every extreme that they name: `lengths`: the longest request fills its cache. `destination`: a permutation of the replicas without fixed points.
All inputs are finite; a program needn't handle non-finite values.
Results may differ from a plain program's by a relative error of at most 0.0065.
Values may be sent and summed in bfloat16 or wider, within the bound.
No kernel may reach another device: no remote copies, remote signals or barrier semaphores. Data moves between devices by JAX's collectives and lax.ppermute only.
A program may use at most 64 MiB of HBM per device.

v0:
```python
import math

import jax
import jax.numpy as jnp
from jax import lax
from jax.sharding import PartitionSpec as P

BLOCK = 32


def combined_all(value, axis, join):
    pieces = jax.tree.map(lambda part: lax.all_gather(part, axis), value)
    head = jax.tree.map(lambda part: part[0], pieces)
    tail = jax.tree.map(lambda part: part[1:], pieces)
    subtotal, _ = lax.scan(lambda subtotal, share: (join(subtotal, share), None), head, tail)
    return subtotal


def combine(first, second):
    first_max, first_total, first_sum = first
    second_max, second_total, second_sum = second
    joint_max = jnp.maximum(first_max, second_max)
    first_scale = jnp.exp(first_max - joint_max)
    second_scale = jnp.exp(second_max - joint_max)
    return (
        joint_max,
        first_total * first_scale + second_total * second_scale,
        first_sum * first_scale[..., None] + second_sum * second_scale[..., None],
    )


def body(kv_cache, lengths, queries, new_kv, moving_slot, destination, block_index):
    req_dev, kv_pair, pos_dev, width = kv_cache.shape
    steps, req_rows, heads, head_dim = queries.shape
    kv_heads = width // head_dim
    group_size = heads // kv_heads
    tp_count = lax.axis_size("tp")
    rep_count = lax.axis_size("replica")
    tp_rank = lax.axis_index("tp")
    rep_rank = lax.axis_index("replica")
    local_heads = heads // tp_count
    factor = 1.0 / math.sqrt(head_dim)
    positions = tp_rank * pos_dev + lax.iota(jnp.int32, pos_dev)
    live = positions[None, :] < lengths[:, None]
    cache_keys = kv_cache[:, 0].reshape(req_dev, pos_dev, kv_heads, head_dim)
    cache_values = kv_cache[:, 1].reshape(req_dev, pos_dev, kv_heads, head_dim)
    grouped = queries.reshape(steps, req_dev, kv_heads, group_size, head_dim)
    scores = (
        jnp.einsum("srkgd,rpkd->srkgp", grouped, cache_keys, preferred_element_type=jnp.float32)
        * factor
    )
    visible = live[None, :, None, None, :]
    scores = jnp.where(visible, scores, -1e30)
    local_max = jnp.max(scores, axis=-1)
    weights = jnp.where(visible, jnp.exp(scores - local_max[..., None]), 0.0)
    local_total = jnp.sum(weights, axis=-1)
    local_sum = jnp.einsum(
        "srkgp,rpkd->srkgd",
        weights.astype(jnp.bfloat16),
        cache_values,
        preferred_element_type=jnp.float32,
    )
    local_max = local_max.reshape(steps, req_dev, heads)
    local_total = local_total.reshape(steps, req_dev, heads)
    local_sum = local_sum.reshape(steps, req_dev, heads, head_dim)
    head_start = tp_rank * local_heads
    merged = combined_all((local_max, local_total, local_sum), "tp", combine)
    run_max = lax.dynamic_slice_in_dim(merged[0], head_start, local_heads, 2)
    run_total = lax.dynamic_slice_in_dim(merged[1], head_start, local_heads, 2)
    run_sum = lax.dynamic_slice_in_dim(merged[2], head_start, local_heads, 2)
    own_queries = lax.dynamic_slice_in_dim(queries, head_start, local_heads, 2).astype(jnp.float32)
    head_group = (head_start + lax.iota(jnp.int32, local_heads)) // group_size
    picker = (head_group[:, None] == lax.iota(jnp.int32, kv_heads)[None, :]).astype(jnp.float32)
    new_keys = new_kv[:, :, 0].reshape(steps, req_dev, kv_heads, head_dim).astype(jnp.float32)
    new_values = new_kv[:, :, 1].reshape(steps, req_dev, kv_heads, head_dim).astype(jnp.float32)
    head_keys = jnp.einsum("trkd,hk->trhd", new_keys, picker)
    head_values = jnp.einsum("trkd,hk->trhd", new_values, picker).astype(jnp.bfloat16)
    fresh = jnp.einsum("srhd,trhd->srht", own_queries, head_keys) * factor
    causal = lax.iota(jnp.int32, steps)[None, :] <= lax.iota(jnp.int32, steps)[:, None]
    causal = causal[:, None, None, :]
    fresh = jnp.where(causal, fresh, -1e30)
    final_max = jnp.maximum(run_max, jnp.max(fresh, axis=-1))
    keep_scale = jnp.exp(run_max - final_max)
    fresh_weights = jnp.where(causal, jnp.exp(fresh - final_max[..., None]), 0.0)
    final_total = run_total * keep_scale + jnp.sum(fresh_weights, axis=-1)
    final_sum = run_sum * keep_scale[..., None] + jnp.einsum(
        "srht,trhd->srhd",
        fresh_weights.astype(jnp.bfloat16),
        head_values,
        preferred_element_type=jnp.float32,
    )
    attended = (final_sum / final_total[..., None]).astype(jnp.bfloat16)
    mine = moving_slot[0]
    moving = lax.dynamic_slice(
        kv_cache, (mine, 0, block_index[0] * BLOCK, 0), (1, kv_pair, BLOCK, width)
    )
    fresh_own = jnp.moveaxis(lax.dynamic_slice_in_dim(new_kv, mine, 1, 1), 1, 0)
    replica_ids = lax.iota(jnp.int32, rep_count)
    source = jnp.sum(jnp.where(destination == rep_rank, replica_ids, 0))
    empty = (jnp.zeros(moving.shape, jnp.bfloat16), jnp.zeros(fresh_own.shape, jnp.bfloat16))
    blocks = lax.all_gather(moving, "replica", axis=0, tiled=True)
    tokens = lax.all_gather(fresh_own, "replica", axis=0, tiled=True)
    count = blocks.shape[0]
    inside = (source >= 0) & (source < count)
    picked = jnp.clip(source, 0, count - 1)
    block_pick = lax.dynamic_slice_in_dim(blocks, picked, 1, 0)
    token_pick = lax.dynamic_slice_in_dim(tokens, picked, 1, 0)
    arrived = jnp.where(inside, block_pick, empty[0])
    handed = jnp.where(inside, token_pick, empty[1])
    return (attended, arrived, handed)


def solution(mesh):
    placed = (
        P("replica", None, "tp", None),
        P("replica"),
        P(None, "replica", None, None),
        P(None, "replica", None, None),
        P("replica"),
        P(),
        P("replica"),
    )
    return jax.shard_map(
        body,
        mesh=mesh,
        in_specs=placed,
        out_specs=(
            P(None, "replica", "tp", None),
            P("replica", None, "tp", None),
            P("replica", None, None, None),
        ),
        check_vma=False,
    )
```

profile of v0, /device:TPU:1, one launch (start us, length us, event | category | flops | bytes accessed | tf_op | source)
XLA Modules:
  0.0 431.9 jit_solution(15181375972102708076)
XLA Ops:
  7.2 0.0 copy-start
  7.2 0.0 all-gather.6.cloned.1.call-start
  8.6 1.6 constant_dynamic-slice_fusion.1
  10.1 0.0 all-gather.6.cloned.1.call-update
  10.2 0.0 all-gather.4.cloned.1.call-start
  10.2 0.0 copy-start.2
  10.2 1.8 fusion.31
  12.1 0.0 copy-start.3
  12.1 0.0 copy-start.1
  12.1 0.7 copy.94
  12.8 0.7 copy.95
  13.5 0.0 copy-done.2
  13.5 0.1 broadcast_compare_fusion
  13.5 0.0 copy-done
  13.5 0.5 fusion.32
  14.0 0.7 convolution_bitcast_fusion
  14.7 0.8 copy.107
  15.5 0.0 all-gather.4.cloned.1.call-update
  15.6 0.0 copy-done.3
  15.6 0.6 fusion.28
  17.5 0.2 slice_reduce_fusion
  17.8 0.2 convolution_bitcast_fusion.2
  18.0 0.1 fusion.16
  18.1 0.2 copy.76
  18.3 0.1 fusion.20
  18.4 0.1 copy.91
  18.5 0.1 all_gather_reshape.9
  18.6 0.4 fusion.10
  19.0 0.1 all_gather_reshape.10
  19.1 51.2 %all_gather.15 = f32[16,3,4,64]{3,2,1,0:T(4,128)S(1)} all-gather(f32[1,3,4,64]{3,2,1,0:T(4,128)S(1)} %all_gather_reshape.9), channel_id=1, replica_groups=mesh['replica'=32,'tp'=16] {'tp'}, dimensions={0}, use_global_device_ids=true | all-gather | bytes 52224 | tf_op jit(solution)/shard_map/all_gather | solution.py:12
  70.3 34.0 %all_gather.16 = f32[16,3,4,64]{3,2,1,0:T(4,128)S(1)} all-gather(f32[1,3,4,64]{3,2,1,0:T(4,128)S(1)} %all_gather_reshape.10), channel_id=1, replica_groups=mesh['replica'=32,'tp'=16] {'tp'}, dimensions={0}, use_global_device_ids=true | all-gather | bytes 52224 | tf_op jit(solution)/shard_map/all_gather | solution.py:12
  105.1 106.6 %all-gather = bf16[96,1,2,1024]{3,2,1,0:T(2,128)(2,1)S(1)} all-gather(bf16[3,1,2,1024]{3,2,1,0:T(2,128)(2,1)S(1)} %constant_dynamic-slice_fusion), channel_id=2, replica_groups=mesh['replica'=32,'tp'=16] {'replica'}, dimensions={0}, use_global_device_ids=true | all-gather | bytes 405504 | tf_op jit(solution)/shard_map/all_gather | solution.py:102
  211.7 0.6 broadcast_select_fusion
  212.3 0.2 fusion.8
  212.5 12.9 %all-gather.6.cloned.1.call-done = bf16[32,2,32,1024]{3,2,1,0:T(8,128)(2,1)} async-done(((bf16[1,2,32,1024]{3,2,1,0:T(8,128)(2,1)}), bf16[32,2,32,1024]{3,2,1,0:T(8,128)(2,1)}) %all-gather.6.cloned.1.call-update) | async-done | bytes 4194320 | tf_op jit(solution)/shard_map/all_gather | solution.py:101
  225.4 1.6 dynamic-slice_select_fusion
  227.0 167.6 %all-gather.4.cloned.1.call-done = f32[16,3,4,64,128]{4,3,2,1,0:T(8,128)} async-done(((f32[1,3,4,64,128]{4,3,2,1,0:T(8,128)}), f32[16,3,4,64,128]{4,3,2,1,0:T(8,128)}) %all-gather.4.cloned.1.call-update) | async-done | bytes 6291472 | tf_op jit(solution)/shard_map/all_gather | solution.py:12
  394.6 1.0 slice_bitcast_fusion
  395.6 6.2 %slice.45 = f32[15,3,4,64,128]{4,3,2,1,0:T(8,128)} slice(f32[16,3,4,64,128]{4,3,2,1,0:T(8,128)} %all-gather.4.cloned.1.call-done), slice={[1:16], [0:3], [0:4], [0:64], [0:128]} | slice | bytes 11796480 | tf_op jit(solution)/shard_map/slice | solution.py:14
  401.9 21.4 %while.14 = (s32[]{:T(128)}, f32[3,4,64]{2,1,0:T(4,128)S(1)}, f32[3,4,64]{2,1,0:T(4,128)S(1)}, f32[3,4,64,128]{3,2,1,0:T(8,128)S(1)}, f32[15,3,4,64]{3,2,1,0:T(4...) while((s32[]{:T(128)}, f32[3,4,64]{2,1,0:T(4,128)S(1)}, ...), condition=%wide.region_3.4_spmd, body=%wide.region_2.3_spmd.sunk | while | flops 299522 | bytes 1210469 | solution.py:15
  401.9 1.4 fusion.42
  403.3 1.4 fusion.42
  404.7 1.4 fusion.42
  406.2 1.4 fusion.42
  407.6 1.4 fusion.42
  409.0 1.4 fusion.42
  410.5 1.4 fusion.42
  411.9 1.4 fusion.42
  413.3 1.4 fusion.42
  414.7 1.4 fusion.42
  416.2 1.4 fusion.42
  417.6 1.4 fusion.42
  419.0 1.4 fusion.42
  420.4 1.4 fusion.42
  421.9 1.4 fusion.42
  423.3 0.1 copy.73
  423.4 0.1 copy.78
  423.5 0.1 fusion.21
  423.6 0.2 copy.80
  423.8 0.3 copy.72
  424.1 0.1 copy.92
  424.2 0.1 copy.81
  424.3 0.1 fusion.7
  424.5 0.6 copy.83
  (31 shorter events, 0.6 us)
Async XLA Ops:
  7.2 6.4 %copy-start = (bf16[3,4,64,128]{3,2,1,0:T(8,128)(2,1)S(1)}, bf16[3,4,64,128]{3,2,1,0:T(8,128)(2,1)}, u32[]{:S(2)}) copy-start(bf16[3,4,64,128]{3,2,1,0:T(8,128)(2,1)} %param.11) | copy-start | bytes 589828
  7.2 218.2 %all-gather.6.cloned.1.call-start = ((), (), s32[]{:S(2)}) async-start(), calls=%async_computation.1 | async-start | bytes 4325376 | tf_op jit(solution)/shard_map/all_gather | solution.py:101
  10.2 384.4 %all-gather.4.cloned.1.call-start = ((), (), s32[]{:S(2)}) async-start(), calls=%async_computation | async-start | bytes 6684672 | tf_op jit(solution)/shard_map/all_gather | solution.py:12
  10.2 3.2 copy-start.2
  12.1 3.5 copy-start.3
  12.1 5.4 %copy-start.1 = (bf16[3,4,2,1024]{3,2,1,0:T(2,128)(2,1)S(1)}, bf16[3,4,2,1024]{3,2,1,0:T(2,128)(2,1)}, u32[]{:S(2)}) copy-start(bf16[3,4,2,1024]{3,2,1,0:T(2,128)(2,1)} %param.12) | copy-start | bytes 147460
Sparse Core Ops, SparseCore 0:
  10.7 214.6 all-gather.5
  228.7 165.8 all-gather.3
where the time goes:
time: 433 us; the launch traced here: 432 us
  blocking collectives  192 us (44%)
  waiting for transfers between devices  181 us (42%)
  other arithmetic  24.6 us (6%)
  between operations  17.6 us (4%)
  local copies, waits for them, and re-layouts  15.1 us (3%)
    all_gather x1, waiting for transfers between devices, combined_all(): pieces = jax.tree.map(lambda part: lax.all_gather(part, axis), value)  168 us
    all_gather x1, blocking collectives, body(): tokens = lax.all_gather(fresh_own, 'replica', axis=0, tiled=True)  107 us
    all_gather x2, blocking collectives, combined_all(): pieces = jax.tree.map(lambda part: lax.all_gather(part, axis), value)  85.2 us
    add x15, other arithmetic, combine(): first_sum * first_scale[..., None] + second_sum * second_scale[..., None]  20.7 us
    all_gather x1, waiting for transfers between devices, body(): blocks = lax.all_gather(moving, 'replica', axis=0, tiled=True)  12.9 us
  transfers between devices with their start and end apart: 2, of which 2 were waited for; matrix products, arithmetic and copies ran while one was open for 2% of the time, Pallas kernels for 0%

commit v1 on v0

v1 whole, which is shorter than its diff:
```python
import functools
import math

import jax
import jax.numpy as jnp
from jax import lax
from jax.experimental import pallas as pl
from jax.experimental.pallas import tpu as pltpu
from jax.sharding import PartitionSpec as P

BLOCK = 32
HALF = 16
SLOT = 40
LANES = 128
HIDDEN = -1e30


def pack_kernel(slot_ref, block_ref, cache_ref, token_ref, out_ref):
    row = lax.broadcasted_iota(jnp.int32, (8, LANES), 0)
    for pair in range(2):
        for tile in range(8):
            columns = pl.ds(tile * LANES, LANES)
            piece = cache_ref[0, pair, :, columns]
            tokens = jnp.zeros((8, LANES), jnp.float32)
            for step in range(3):
                line = token_ref[step, 0, :, columns].astype(jnp.float32)[pair : pair + 1]
                tokens = jnp.where(row == step, line, tokens)
            whole = jnp.concatenate([piece.astype(jnp.float32), tokens], axis=0).astype(jnp.bfloat16)
            for half in range(2):
                out_ref[half * HALF + pair * 8 + tile] = whole


def pack(kv_cache, new_kv, moving_slot, block_index):
    width = kv_cache.shape[-1]
    return pl.pallas_call(
        pack_kernel,
        grid_spec=pltpu.PrefetchScalarGridSpec(
            num_scalar_prefetch=2,
            grid=(1,),
            in_specs=[
                pl.BlockSpec((1, 2, BLOCK, width), lambda i, slot, block: (slot[0], 0, block[0], 0)),
                pl.BlockSpec((3, 1, 2, width), lambda i, slot, block: (0, slot[0], 0, 0)),
            ],
            out_specs=pl.BlockSpec((2 * HALF, SLOT, LANES), lambda i, slot, block: (0, 0, 0)),
        ),
        out_shape=jax.ShapeDtypeStruct((2 * HALF, SLOT, LANES), jnp.bfloat16),
        cost_estimate=pl.CostEstimate(flops=0, bytes_accessed=1 << 20, transcendentals=0),
        name="pack",
    )(moving_slot, block_index, kv_cache, new_kv)


def reorder_kernel(destination_ref, mine_ref, in_ref, out_ref, source_ref):
    for source in range(2 * HALF):
        source_ref[destination_ref[source]] = source
    base = mine_ref[0] // HALF * HALF
    for slot in range(HALF):
        out_ref[slot] = in_ref[source_ref[base + slot]]


def reorder(destination, mine, pieces):
    return pl.pallas_call(
        reorder_kernel,
        grid_spec=pltpu.PrefetchScalarGridSpec(
            num_scalar_prefetch=2,
            grid=(1,),
            in_specs=[pl.BlockSpec((2 * HALF, SLOT, LANES), lambda i, a, b: (0, 0, 0))],
            out_specs=pl.BlockSpec((HALF, SLOT, LANES), lambda i, a, b: (0, 0, 0)),
            scratch_shapes=[pltpu.SMEM((2 * HALF,), jnp.int32)],
        ),
        out_shape=jax.ShapeDtypeStruct((HALF, SLOT, LANES), jnp.bfloat16),
        cost_estimate=pl.CostEstimate(flops=0, bytes_accessed=1 << 20, transcendentals=0),
        name="reorder",
    )(destination, mine, pieces)


def unpack_kernel(in_ref, arrived_ref, handed_ref):
    row = lax.broadcasted_iota(jnp.int32, (2, LANES), 0)
    for tile in range(8):
        columns = pl.ds(tile * LANES, LANES)
        lines = []
        for pair in range(2):
            whole = in_ref[pair * 8 + tile].astype(jnp.float32)
            arrived_ref[0, pair, :, columns] = whole[:BLOCK].astype(jnp.bfloat16)
            lines.append(whole[BLOCK:])
        for step in range(3):
            both = jnp.where(row == 0, lines[0][step : step + 1], lines[1][step : step + 1])
            handed_ref[0, step, :, columns] = both.astype(jnp.bfloat16)


def unpack(pieces, width):
    return pl.pallas_call(
        unpack_kernel,
        in_specs=[pl.BlockSpec(memory_space=pltpu.VMEM)],
        out_specs=[pl.BlockSpec(memory_space=pltpu.VMEM)] * 2,
        out_shape=(
            jax.ShapeDtypeStruct((1, 2, BLOCK, width), jnp.bfloat16),
            jax.ShapeDtypeStruct((1, 3, 2, width), jnp.bfloat16),
        ),
        cost_estimate=pl.CostEstimate(flops=0, bytes_accessed=1 << 20, transcendentals=0),
        name="unpack",
    )(pieces)


def partial_kernel(lengths_ref, rank_ref, cache_ref, query_ref, out_ref):
    request = pl.program_id(0)
    factor = 1.0 / math.sqrt(LANES)
    pos_dev = cache_ref.shape[2]
    position = rank_ref[0] * pos_dev + lax.broadcasted_iota(jnp.int32, (32, pos_dev), 1)
    live = position < lengths_ref[request]
    row8 = lax.broadcasted_iota(jnp.int32, (8, LANES), 0)
    top = row8 < 4
    row = lax.broadcasted_iota(jnp.int32, (32, LANES), 0) % 16
    lane = lax.broadcasted_iota(jnp.int32, (32, LANES), 1)
    group = lane // 16
    diagonal = lane % 16 == row
    steps = [query_ref[step, 0].astype(jnp.float32) for step in range(3)]
    for head in range(8):
        q0, q1, q2 = (part[head * 8 : head * 8 + 8] for part in steps)
        rolled0, rolled1, rolled2 = (pltpu.roll(part, 4, 0) for part in (q0, q1, q2))
        zero = jnp.zeros_like(q0)
        query = jnp.concatenate(
            [
                jnp.where(top, q0, rolled1),
                jnp.where(top, q2, zero),
                jnp.where(top, rolled0, q1),
                jnp.where(top, rolled2, zero),
            ],
            axis=0,
        ).astype(jnp.bfloat16)
        columns = pl.ds(head * LANES, LANES)
        scores = lax.dot_general(
            query,
            cache_ref[0, 0, :, columns],
            (((1,), (1,)), ((), ())),
            preferred_element_type=jnp.float32,
        )
        scores = jnp.where(live, scores * factor, HIDDEN)
        top_score = jnp.max(scores, axis=1, keepdims=True)
        weights = jnp.where(live, jnp.exp(scores - top_score), 0.0)
        total = jnp.sum(weights, axis=1, keepdims=True)
        summed = jnp.dot(
            weights.astype(jnp.bfloat16),
            cache_ref[0, 1, :, columns],
            preferred_element_type=jnp.float32,
        )
        max_high = top_score.astype(jnp.bfloat16).astype(jnp.float32)
        rest = top_score - max_high
        max_mid = rest.astype(jnp.bfloat16).astype(jnp.float32)
        max_low = rest - max_mid
        total_high = total.astype(jnp.bfloat16).astype(jnp.float32)
        total_low = total - total_high
        stats = jnp.where(group == 0, max_high, 0.0)
        stats = jnp.where(group == 1, max_mid, stats)
        stats = jnp.where(group == 2, max_low, stats)
        stats = jnp.where(group == 3, total_high, stats)
        stats = jnp.where(group == 4, total_low, stats)
        stats = jnp.where(diagonal, stats, 0.0)
        for half in range(2):
            rows = slice(half * 16, half * 16 + 16)
            line = jnp.sum(stats[rows], axis=0, keepdims=True)
            chunk = jnp.where(row[rows] == 12, line, summed[rows])
            out_ref[2 * head + half, 0] = chunk.astype(jnp.bfloat16)


def partials(kv_cache, queries, lengths, rank):
    req_dev, pair, pos_dev, width = kv_cache.shape
    steps, _, heads, head_dim = queries.shape
    return pl.pallas_call(
        partial_kernel,
        grid_spec=pltpu.PrefetchScalarGridSpec(
            num_scalar_prefetch=2,
            grid=(req_dev,),
            in_specs=[
                pl.BlockSpec((1, pair, pos_dev, width), lambda r, a, b: (r, 0, 0, 0)),
                pl.BlockSpec((steps, 1, heads, head_dim), lambda r, a, b: (0, r, 0, 0)),
            ],
            out_specs=pl.BlockSpec((16, 1, 16, LANES), lambda r, a, b: (0, r, 0, 0)),
        ),
        out_shape=jax.ShapeDtypeStruct((16, req_dev, 16, LANES), jnp.bfloat16),
        cost_estimate=pl.CostEstimate(
            flops=4 * 32 * 8 * req_dev * pos_dev * head_dim,
            bytes_accessed=12 << 20,
            transcendentals=32 * 8 * req_dev * pos_dev,
        ),
        name="partials",
    )(lengths, rank, kv_cache, queries)


def merge_kernel(rank_ref, chunk_ref, query_ref, token_ref, out_ref):
    rank = rank_ref[0]
    kv_head = rank // 2
    factor = 1.0 / math.sqrt(LANES)
    sources = chunk_ref.shape[0]
    row = lax.broadcasted_iota(jnp.int32, (16, LANES), 0)
    lane = lax.broadcasted_iota(jnp.int32, (16, LANES), 1)
    diagonal = lane % 16 == row
    spread_group = lax.broadcasted_iota(jnp.int32, (LANES, 2 * LANES), 0) // 16
    spread_total = lax.broadcasted_iota(jnp.int32, (LANES, 2 * LANES), 1) >= LANES
    spread = jnp.where(
        spread_total,
        jnp.where((spread_group == 3) | (spread_group == 4), 1.0, 0.0),
        jnp.where(spread_group < 3, 1.0, 0.0),
    ).astype(jnp.bfloat16)
    row8 = lax.broadcasted_iota(jnp.int32, (8, LANES), 0)
    columns = pl.ds(pl.multiple_of(kv_head * LANES, LANES), LANES)
    for request in range(chunk_ref.shape[1]):
        chunks = [chunk_ref[source, request].astype(jnp.float32) for source in range(sources)]
        lines = [jnp.where(diagonal, chunk[12:13], 0.0) for chunk in chunks]
        stats = jnp.dot(
            jnp.concatenate(lines, axis=0).astype(jnp.bfloat16),
            spread,
            preferred_element_type=jnp.float32,
        )
        tops = [stats[16 * source : 16 * source + 16, :LANES] for source in range(sources)]
        totals = [stats[16 * source : 16 * source + 16, LANES:] for source in range(sources)]
        parts = []
        for step in range(3):
            pair = query_ref[step, request, pl.ds(pl.multiple_of(rank // 4 * 16, 16), 16), :]
            pair = pair.astype(jnp.float32)
            tile = jnp.where((rank // 2) % 2 == 1, pair[8:], pair[:8])
            parts.append(jnp.where(rank % 2 == 1, pltpu.roll(tile, 4, 0), tile))
        query = jnp.concatenate(
            [jnp.where(row8 < 4, parts[0], pltpu.roll(parts[1], 4, 0)), parts[2]], axis=0
        )
        scores, values = [], []
        for step in range(3):
            token = token_ref[step, request, :, columns].astype(jnp.float32)
            score = jnp.sum(query * token[0:1], axis=1, keepdims=True) * factor
            scores.append(jnp.where(row >= 4 * step, score, HIDDEN))
            values.append(token[1:2])
        joint = functools.reduce(jnp.maximum, tops + scores)
        total = jnp.zeros((16, LANES), jnp.float32)
        summed = jnp.zeros((16, LANES), jnp.float32)
        for source in range(sources):
            scale = jnp.exp(tops[source] - joint)
            total += totals[source] * scale
            summed += chunks[source] * scale
        for step in range(3):
            weight = jnp.where(row >= 4 * step, jnp.exp(scores[step] - joint), 0.0)
            total += weight
            summed += weight.astype(jnp.bfloat16).astype(jnp.float32) * values[step]
        attended = summed / total
        for step in range(3):
            out_ref[step, request] = attended[4 * step : 4 * step + 4].astype(jnp.bfloat16)


def merge(rank, chunks, queries, new_kv):
    steps, req_dev, _, head_dim = queries.shape
    return pl.pallas_call(
        merge_kernel,
        in_specs=[pl.BlockSpec(memory_space=pltpu.SMEM)] + [pl.BlockSpec(memory_space=pltpu.VMEM)] * 3,
        out_specs=pl.BlockSpec(memory_space=pltpu.VMEM),
        out_shape=jax.ShapeDtypeStruct((steps, req_dev, 4, head_dim), jnp.bfloat16),
        cost_estimate=pl.CostEstimate(flops=0, bytes_accessed=6 << 20, transcendentals=0),
        name="merge",
    )(rank, chunks, queries, new_kv)


def body(kv_cache, lengths, queries, new_kv, moving_slot, destination, block_index):
    rank = lax.axis_index("tp").astype(jnp.int32)[None]
    mine = lax.axis_index("replica").astype(jnp.int32)[None]
    sent = pack(kv_cache, new_kv, moving_slot, block_index)
    pieces = lax.all_to_all(sent, "replica", 0, 0, tiled=True)
    local = partials(kv_cache, queries, lengths, rank)
    chunks = lax.all_to_all(local, "tp", 0, 0, tiled=True)
    ordered = reorder(destination, mine, pieces)
    halves = [list(range(HALF)), list(range(HALF, 2 * HALF))]
    delivered = lax.all_to_all(ordered, "replica", 0, 0, tiled=True, axis_index_groups=halves)
    attended = merge(rank, chunks, queries, new_kv)
    arrived, handed = unpack(delivered, kv_cache.shape[-1])
    return (attended, arrived, handed)


def solution(mesh):
    placed = (
        P("replica", None, "tp", None),
        P("replica"),
        P(None, "replica", None, None),
        P(None, "replica", None, None),
        P("replica"),
        P(),
        P("replica"),
    )
    return jax.shard_map(
        body,
        mesh=mesh,
        in_specs=placed,
        out_specs=(
            P(None, "replica", "tp", None),
            P("replica", None, "tp", None),
            P("replica", None, None, None),
        ),
        check_vma=False,
    )
```

time: 433 us -> 90.4 us (0.21)
  blocking collectives: 192 us -> 0 us
  waiting for transfers between devices: 181 us -> 27.7 us
  starting transfers between devices: 0.08 us -> 41.5 us
  other arithmetic: 24.6 us -> 0 us
  Pallas kernels: 0 us -> 18.1 us
  between operations: 17.6 us -> 1.96 us
  local copies, waits for them, and re-layouts: 15.1 us -> 0.66 us
    all_gather x3 -> x0, blocking collectives: 192 us -> none  [the longest x1 107 us: body(): tokens = lax.all_gather(fresh_own, 'replica', axis=0, tiled=True)]
    all_gather x2 -> x0, waiting for transfers between devices: 181 us -> none  [the longest x1 168 us: combined_all(): pieces = jax.tree.map(lambda part: lax.all_gather(part, axis), value)]
    all_to_all x0 -> x3, starting transfers between devices: none -> 41.5 us  [the longest x1 15.9 us: body(): pieces = lax.all_to_all(sent, 'replica', 0, 0, tiled=True)]
    all_to_all x0 -> x3, waiting for transfers between devices: none -> 27.7 us  [the longest x1 13.8 us: body(): chunks = lax.all_to_all(local, 'tp', 0, 0, tiled=True)]
    add x32 -> x0, other arithmetic: 21.1 us -> none  [the longest x15 20.7 us: combine(): first_sum * first_scale[..., None] + second_sum * second_scale[..., None]]
    pallas_call x0 -> x5, Pallas kernels: none -> 18.1 us  [the longest x1 10.4 us: partials(): pl.pallas_call(partial_kernel, grid_spec=pltpu.PrefetchScalarGridSpec(num...]
    slice x5 -> x0, local copies, waits for them, and re-layouts: 8.3 us -> none  [the longest x3 6.26 us: combined_all(): tail = jax.tree.map(lambda part: part[1:], pieces)]
  transfers between devices with their start and end apart: 2 -> 3, of which waited for: 2 -> 3; matrix products, arithmetic and copies ran while one was open for 2% -> 0% of each run, Pallas kernels for 0% -> 16%
where the time goes in v1:
time: 90.4 us; the launch traced here: 89.9 us
  starting transfers between devices  41.5 us (46%)
  waiting for transfers between devices  27.7 us (31%)
  Pallas kernels  18.1 us (20%)
  between operations  1.96 us (2%)
    all_to_all x1, starting transfers between devices, body(): pieces = lax.all_to_all(sent, 'replica', 0, 0, tiled=True)  15.9 us
    all_to_all x1, starting transfers between devices, body(): chunks = lax.all_to_all(local, 'tp', 0, 0, tiled=True)  14.6 us
    all_to_all x1, waiting for transfers between devices, body(): chunks = lax.all_to_all(local, 'tp', 0, 0, tiled=True)  13.8 us
    all_to_all x1, starting transfers between devices, body(): lax.all_to_all(ordered, 'replica', 0, 0, tiled=True, axis_index_groups=ha...  10.9 us
    pallas_call x1, Pallas kernels, partials(): pl.pallas_call(partial_kernel, grid_spec=pltpu.PrefetchScalarGridSpec(num...  10.4 us
    all_to_all x1, waiting for transfers between devices, body(): pieces = lax.all_to_all(sent, 'replica', 0, 0, tiled=True)  7.9 us
    all_to_all x1, waiting for transfers between devices, body(): lax.all_to_all(ordered, 'replica', 0, 0, tiled=True, axis_index_groups=ha...  5.96 us
    pallas_call x1, Pallas kernels, reorder(): pl.pallas_call(reorder_kernel, grid_spec=pltpu.PrefetchScalarGridSpec(num...  2.32 us
  transfers between devices with their start and end apart: 3, of which 3 were waited for; matrix products, arithmetic and copies ran while one was open for 0% of the time, Pallas kernels for 16%

profile of v1, /device:TPU:1, one launch (start us, length us, event | category | flops | bytes accessed | tf_op | source)
XLA Modules:
  0.0 89.9 jit_solution(868311616653890760)
XLA Ops:
  1.9 1.7 %pack.1 = bf16[32,40,128]{2,1,0:T(8,128)(2,1)} custom-call(s32[1]{0:T(128)S(6)} %copy.10.slot_ref, s32[1]{0:T(128)S(6)} %copy.11.block_ref, bf16[4,2,128,1024]{3,2,1,0:T(8,128)(2,1)} %cache_ref.3, bf16[3,4,2,1024]{3,2,1,0:T(2,128)(2,1)} %token_ref.3), custom_call_target="tpu_custom_call" | custom-call | bytes 1048576 | tf_op jit(solution)/shard_map/pack/pallas_call | solution.py:35
  3.6 15.9 %all-to-all-start.1 = ((bf16[32,40,128]{2,1,0:T(8,128)(2,1)}), bf16[32,40,128]{2,1,0:T(8,128)(2,1)S(1)}, u32[]{:S(2)}, u32[]{:S(2)}) async-start(bf16[32,40,128]{2,1,0:T(8,128)(2,1)} %pack.1), calls=%async_computation.1 | async-start | bytes 655360 | tf_op jit(solution)/shard_map/all_to_all | solution.py:263
  19.5 10.4 %partials.1 = bf16[16,4,16,128]{3,2,1,0:T(8,128)(2,1)} custom-call(s32[4]{0:T(128)} %lengths_ref.1, s32[1]{0:T(128)} %bitcast.rank_ref, bf16[4,2,128,1024]{3,2,1,0:T(8,128)(2,1)} %cache_ref.3, bf16[3,4,64,128]{3,2,1,0:T(8,128)(2,1)} %query_ref.3), custom_call_target="tpu_custom_call" | custom-call | flops 67108864 | bytes 12582912 | tf_op jit(solution)/shard_map/partials/pallas_call | solution.py:168
  29.9 7.9 %all-to-all-done.1.in_ref = bf16[32,40,128]{2,1,0:T(8,128)(2,1)S(1)} async-done(((bf16[32,40,128]{2,1,0:T(8,128)(2,1)}), bf16[32,40,128]{2,1,0:T(8,128)(2,1)S(1)}, u32[]{:S(2)}, u32[]{:S(2)}) %all-to-all-start.1) | async-done | bytes 327712 | tf_op jit(solution)/shard_map/all_to_all | solution.py:263
  37.8 0.0 copy-start
  37.8 14.6 %all-to-all-start = ((bf16[16,4,16,128]{3,2,1,0:T(8,128)(2,1)}), bf16[16,4,16,128]{3,2,1,0:T(8,128)(2,1)S(1)}, u32[]{:S(2)}, u32[]{:S(2)}) async-start(bf16[16,4,16,128]{3,2,1,0:T(8,128)(2,1)} %partials.1), calls=%async_computation | async-start | bytes 524288 | tf_op jit(solution)/shard_map/all_to_all | solution.py:265
  52.5 0.0 copy-done
  52.5 2.3 %reorder.1 = bf16[16,40,128]{2,1,0:T(8,128)(2,1)} custom-call(s32[32]{0:T(128)} %destination_ref.1, s32[1]{0:T(128)} %bitcast.1.mine_ref, bf16[32,40,128]{2,1,0:T(8,128)(2,1)} %copy-done), custom_call_target="tpu_custom_call" | custom-call | bytes 1048576 | tf_op jit(solution)/shard_map/reorder/pallas_call | solution.py:61
  54.8 13.8 %all-to-all-done.chunk_ref = bf16[16,4,16,128]{3,2,1,0:T(8,128)(2,1)S(1)} async-done(((bf16[16,4,16,128]{3,2,1,0:T(8,128)(2,1)}), bf16[16,4,16,128]{3,2,1,0:T(8,128)(2,1)S(1)}, u32[]{:S(2)}, u32[]{:S(2)}) %all-to-all-start) | async-done | bytes 262176 | tf_op jit(solution)/shard_map/all_to_all | solution.py:265
  68.7 0.0 copy-start.1
  68.7 10.9 %all-to-all-start.2 = ((bf16[16,40,128]{2,1,0:T(8,128)(2,1)}), bf16[16,40,128]{2,1,0:T(8,128)(2,1)S(1)}, u32[]{:S(2)}, u32[]{:S(2)}) async-start(bf16[16,40,128]{2,1,0:T(8,128)(2,1)} %reorder.1), calls=%async_computation.2 | async-start | bytes 327680 | tf_op jit(solution)/shard_map/all_to_all | solution.py:268
  79.6 0.0 copy-done.1
  79.6 2.1 %merge.1 = bf16[3,4,4,128]{3,2,1,0:T(4,128)(2,1)} custom-call(s32[1]{0:T(128)} %bitcast.rank_ref, bf16[16,4,16,128]{3,2,1,0:T(8,128)(2,1)} %copy-done.1, bf16[3,4,64,128]{3,2,1,0:T(8,128)(2,1)} %query_ref.3, bf16[3,4,2,1024]{3,2,1,0:T(2,128)(2,1)} %token_ref.3), custom_call_target="tpu_custom_call" | custom-call | bytes 6291456 | tf_op jit(solution)/shard_map/merge/pallas_call | solution.py:249
  81.6 6.0 %all-to-all-done.2.in_ref = bf16[16,40,128]{2,1,0:T(8,128)(2,1)S(1)} async-done(((bf16[16,40,128]{2,1,0:T(8,128)(2,1)}), bf16[16,40,128]{2,1,0:T(8,128)(2,1)S(1)}, u32[]{:S(2)}, u32[]{:S(2)}) %all-to-all-start.2) | async-done | bytes 163872 | tf_op jit(solution)/shard_map/all_to_all | solution.py:268
  87.6 0.0 copy-start.2
  87.6 0.7 copy-done.2
  88.3 1.6 %unpack.1 = (bf16[1,2,32,1024]{3,2,1,0:T(8,128)(2,1)}, bf16[1,3,2,1024]{3,2,1,0:T(2,128)(2,1)}) custom-call(bf16[16,40,128]{2,1,0:T(8,128)(2,1)} %copy-done.2), custom_call_target="tpu_custom_call" | custom-call | bytes 1048576 | tf_op jit(solution)/shard_map/unpack/pallas_call | solution.py:91
Async XLA Ops:
  3.6 34.2 %all-to-all-start.1 = ((bf16[32,40,128]{2,1,0:T(8,128)(2,1)}), bf16[32,40,128]{2,1,0:T(8,128)(2,1)S(1)}, u32[]{:S(2)}, u32[]{:S(2)}) async-start(bf16[32,40,128]{2,1,0:T(8,128)(2,1)} %pack.1), calls=%async_computation.1 | async-start | bytes 655360 | tf_op jit(solution)/shard_map/all_to_all | solution.py:263
  37.8 14.7 %copy-start = (bf16[32,40,128]{2,1,0:T(8,128)(2,1)}, bf16[32,40,128]{2,1,0:T(8,128)(2,1)S(1)}, u32[]{:S(2)}) copy-start(bf16[32,40,128]{2,1,0:T(8,128)(2,1)S(1)} %all-to-all-done.1.in_ref) | copy-start | bytes 983044
  37.8 30.8 %all-to-all-start = ((bf16[16,4,16,128]{3,2,1,0:T(8,128)(2,1)}), bf16[16,4,16,128]{3,2,1,0:T(8,128)(2,1)S(1)}, u32[]{:S(2)}, u32[]{:S(2)}) async-start(bf16[16,4,16,128]{3,2,1,0:T(8,128)(2,1)} %partials.1), calls=%async_computation | async-start | bytes 524288 | tf_op jit(solution)/shard_map/all_to_all | solution.py:265
  68.7 10.9 %copy-start.1 = (bf16[16,4,16,128]{3,2,1,0:T(8,128)(2,1)}, bf16[16,4,16,128]{3,2,1,0:T(8,128)(2,1)S(1)}, u32[]{:S(2)}) copy-start(bf16[16,4,16,128]{3,2,1,0:T(8,128)(2,1)S(1)} %all-to-all-done.chunk_ref) | copy-start | bytes 786436
  68.7 18.9 %all-to-all-start.2 = ((bf16[16,40,128]{2,1,0:T(8,128)(2,1)}), bf16[16,40,128]{2,1,0:T(8,128)(2,1)S(1)}, u32[]{:S(2)}, u32[]{:S(2)}) async-start(bf16[16,40,128]{2,1,0:T(8,128)(2,1)} %reorder.1), calls=%async_computation.2 | async-start | bytes 327680 | tf_op jit(solution)/shard_map/all_to_all | solution.py:268
  87.6 0.7 copy-start.2

commit v2 on v0

v2 whole, which is shorter than its diff:
```python
import functools
import math

import jax
import jax.numpy as jnp
from jax import lax
from jax.experimental import pallas as pl
from jax.experimental.pallas import tpu as pltpu
from jax.sharding import PartitionSpec as P

BLOCK = 32
HALF = 16
SLOT = 40
CHUNK = 56
LANES = 128
HIDDEN = -1e30
FACTOR = 1.0 / math.sqrt(LANES)
LIMIT = 16 << 20
FRONT_LIMIT = 61 << 20


def front_kernel(
    place_ref, lengths_hbm, cache_hbm, query_hbm, local_ref,
    lengths_ref, cache_ref, query_ref, lengths_sem, cache_sem, query_sem,
):
    requests, _, pos_dev, _ = cache_ref.shape
    lengths_copy = pltpu.make_async_copy(lengths_hbm, lengths_ref, lengths_sem)
    lengths_copy.start()
    query_copy = pltpu.make_async_copy(query_hbm, query_ref, query_sem)
    query_copy.start()
    cache_copies = [
        pltpu.make_async_copy(cache_hbm.at[r], cache_ref.at[r], cache_sem.at[r]) for r in range(requests)
    ]
    for copy in cache_copies:
        copy.start()

    position = place_ref[0] * pos_dev + lax.broadcasted_iota(jnp.int32, (8, pos_dev), 1)
    lane = lax.broadcasted_iota(jnp.int32, (8, LANES), 1)
    top = lax.broadcasted_iota(jnp.int32, (8, LANES), 0) < 4
    lengths_copy.wait()
    query_copy.wait()

    def attend(r):
        live = position < lengths_ref[r]
        steps = [query_ref[step, r].astype(jnp.float32) for step in range(3)]
        scores = []
        for head in range(8):
            query = jnp.concatenate([part[head * 8 : head * 8 + 8] for part in steps], axis=0)
            scores.append(
                lax.dot_general(
                    query.astype(jnp.bfloat16),
                    cache_ref[r, 0, :, head * LANES : (head + 1) * LANES],
                    (((1,), (1,)), ((), ())),
                    preferred_element_type=jnp.float32,
                )
            )
        results = []
        for head in range(8):
            tiles, stats = [], []
            for step in range(3):
                score = jnp.where(live, scores[head][8 * step : 8 * step + 8] * FACTOR, HIDDEN)
                peak = jnp.max(score, axis=1, keepdims=True)
                weight = jnp.where(live, jnp.exp(score - peak), 0.0)
                total = jnp.sum(weight, axis=1, keepdims=True)
                tiles.append(weight)
                peak_high = peak.astype(jnp.bfloat16).astype(jnp.float32)
                rest = peak - peak_high
                peak_mid = rest.astype(jnp.bfloat16).astype(jnp.float32)
                total_high = total.astype(jnp.bfloat16).astype(jnp.float32)
                stats.append((peak_high, peak_mid, rest - peak_mid, total_high, total - total_high))
            summed = jnp.dot(
                jnp.concatenate(tiles, axis=0).astype(jnp.bfloat16),
                cache_ref[r, 1, :, head * LANES : (head + 1) * LANES],
                preferred_element_type=jnp.float32,
            )
            results.append((summed, stats))
        return results

    for pair in range(2):
        both = []
        for r in (2 * pair, 2 * pair + 1):
            cache_copies[r].wait()
            both.append(attend(r))
        for head in range(8):
            (sum_a, stats_a), (sum_b, stats_b) = both[0][head], both[1][head]
            table_a = jnp.zeros((8, LANES), jnp.float32)
            table_b = jnp.zeros((8, LANES), jnp.float32)
            for step in range(3):
                a, b = sum_a[8 * step : 8 * step + 8], sum_b[8 * step : 8 * step + 8]
                rows = slice(16 * step + 8 * pair, 16 * step + 8 * pair + 8)
                here = (2 * head % 8, head // 4, rows)
                local_ref[here] = jnp.where(top, a, pltpu.roll(b, 4, 0)).astype(jnp.bfloat16)
                here = (2 * head % 8 + 1, head // 4, rows)
                local_ref[here] = jnp.where(top, pltpu.roll(a, 4, 0), b).astype(jnp.bfloat16)
                for term in range(5):
                    here = lane == (step * 2 + pair) * 8 + term
                    table_a = jnp.where(here, stats_a[step][term], table_a)
                    table_b = jnp.where(here, stats_b[step][term], table_b)
            for half, table in (
                (0, jnp.where(top, table_a, pltpu.roll(table_b, 4, 0))),
                (1, jnp.where(top, pltpu.roll(table_a, 4, 0), table_b)),
            ):
                here = (2 * head % 8 + half, head // 4, slice(48, CHUNK))
                if pair == 1:
                    table = table + local_ref[here].astype(jnp.float32)
                local_ref[here] = table.astype(jnp.bfloat16)


def front(place, lengths, kv_cache, queries):
    req_dev = kv_cache.shape[0]
    return pl.pallas_call(
        front_kernel,
        in_specs=[pl.BlockSpec(memory_space=pltpu.SMEM)] + [pl.BlockSpec(memory_space=pl.ANY)] * 3,
        out_specs=pl.BlockSpec(memory_space=pltpu.VMEM),
        out_shape=jax.ShapeDtypeStruct((8, 2, CHUNK, LANES), jnp.bfloat16),
        scratch_shapes=[
            pltpu.SMEM(lengths.shape, jnp.int32),
            pltpu.VMEM(kv_cache.shape, jnp.bfloat16),
            pltpu.VMEM(queries.shape, jnp.bfloat16),
            pltpu.SemaphoreType.DMA(()),
            pltpu.SemaphoreType.DMA((req_dev,)),
            pltpu.SemaphoreType.DMA(()),
        ],
        compiler_params=pltpu.CompilerParams(vmem_limit_bytes=FRONT_LIMIT),
        name="front",
    )(place, lengths, kv_cache, queries)


def spread_of(index):
    term = lax.broadcasted_iota(jnp.int32, (LANES, 2 * LANES), 0) - index * 8
    second = lax.broadcasted_iota(jnp.int32, (LANES, 2 * LANES), 1) >= LANES
    maxima = jnp.where((term >= 0) & (term < 3), 1.0, 0.0)
    totals = jnp.where((term == 3) | (term == 4), 1.0, 0.0)
    return jnp.where(second, totals, maxima).astype(jnp.bfloat16)


def fold_kernel(
    place_ref, chunk_ref, cache_hbm, token_hbm, sent_ref, out_ref, moving_ref, token_ref, moving_sem, token_sem
):
    slot = place_ref[2]
    first = pl.multiple_of(place_ref[3] * BLOCK, BLOCK)
    moving_copy = pltpu.make_async_copy(cache_hbm.at[slot, :, pl.ds(first, BLOCK)], moving_ref, moving_sem)
    moving_copy.start()
    token_copy = pltpu.make_async_copy(token_hbm, token_ref, token_sem)
    token_copy.start()
    other = 1 - place_ref[0] // 8
    sources = chunk_ref.shape[0]
    lane = lax.broadcasted_iota(jnp.int32, (8, LANES), 1)
    tables = jnp.concatenate(
        [chunk_ref[source, other, 48:CHUNK].astype(jnp.float32) for source in range(sources)], axis=0
    ).astype(jnp.bfloat16)
    joined = jnp.zeros((8, LANES), jnp.float32)
    for index in range(6):
        stats = jnp.dot(tables, spread_of(index), preferred_element_type=jnp.float32)
        peaks = [stats[8 * source : 8 * source + 8, :LANES] for source in range(sources)]
        totals = [stats[8 * source : 8 * source + 8, LANES:] for source in range(sources)]
        joint = functools.reduce(jnp.maximum, peaks)
        total = jnp.zeros((8, LANES), jnp.float32)
        summed = jnp.zeros((8, LANES), jnp.float32)
        for source in range(sources):
            scale = jnp.exp(peaks[source] - joint)
            total += totals[source] * scale
            part = chunk_ref[source, other, 8 * index : 8 * index + 8]
            summed += part.astype(jnp.float32) * scale
        out_ref[8 * index : 8 * index + 8] = summed.astype(jnp.bfloat16)
        joint_high = joint.astype(jnp.bfloat16).astype(jnp.float32)
        rest = joint - joint_high
        joint_mid = rest.astype(jnp.bfloat16).astype(jnp.float32)
        total_high = total.astype(jnp.bfloat16).astype(jnp.float32)
        terms = (joint_high, joint_mid, rest - joint_mid, total_high, total - total_high)
        for term, value in enumerate(terms):
            joined = jnp.where(lane == index * 8 + term, value, joined)
    out_ref[48:CHUNK] = joined.astype(jnp.bfloat16)

    token_copy.wait()
    moving_copy.wait()
    row = lax.broadcasted_iota(jnp.int32, (8, LANES), 0)
    lines = [token_ref[step, slot].astype(jnp.float32) for step in range(3)]
    for kind in range(2):
        for tile in range(8):
            columns = slice(tile * LANES, (tile + 1) * LANES)
            tokens = jnp.zeros((8, LANES), jnp.float32)
            for step in range(3):
                tokens = jnp.where(row == step, lines[step][kind : kind + 1, columns], tokens)
            piece, tokens = moving_ref[kind, :, columns], tokens.astype(jnp.bfloat16)
            for half in range(2):
                sent_ref[half * HALF + kind * 8 + tile, :BLOCK] = piece
                sent_ref[half * HALF + kind * 8 + tile, BLOCK:] = tokens


def fold(place, chunks, kv_cache, new_kv):
    return pl.pallas_call(
        fold_kernel,
        in_specs=[
            pl.BlockSpec(memory_space=pltpu.SMEM),
            pl.BlockSpec(memory_space=pltpu.VMEM),
            pl.BlockSpec(memory_space=pl.ANY),
            pl.BlockSpec(memory_space=pl.ANY),
        ],
        out_specs=[pl.BlockSpec(memory_space=pltpu.VMEM)] * 2,
        out_shape=(
            jax.ShapeDtypeStruct((2 * HALF, SLOT, LANES), jnp.bfloat16),
            jax.ShapeDtypeStruct((CHUNK, LANES), jnp.bfloat16),
        ),
        scratch_shapes=[
            pltpu.VMEM((2, BLOCK, kv_cache.shape[-1]), jnp.bfloat16),
            pltpu.VMEM(new_kv.shape, jnp.bfloat16),
            pltpu.SemaphoreType.DMA(()),
            pltpu.SemaphoreType.DMA(()),
        ],
        compiler_params=pltpu.CompilerParams(vmem_limit_bytes=LIMIT),
        name="fold",
    )(place, chunks, kv_cache, new_kv)


def reorder_kernel(place_ref, destination_ref, in_ref, after_ref, out_ref, source_ref):
    del after_ref
    for source in range(2 * HALF):
        source_ref[destination_ref[source]] = source
    base = place_ref[1] // HALF * HALF
    for slot in range(HALF):
        out_ref[slot] = in_ref[source_ref[base + slot]]


def reorder(place, destination, pieces, after):
    return pl.pallas_call(
        reorder_kernel,
        in_specs=[pl.BlockSpec(memory_space=pltpu.SMEM)] * 2
        + [pl.BlockSpec(memory_space=pltpu.VMEM), pl.BlockSpec(memory_space=pl.ANY)],
        out_specs=pl.BlockSpec(memory_space=pltpu.VMEM),
        out_shape=jax.ShapeDtypeStruct((HALF, SLOT, LANES), jnp.bfloat16),
        scratch_shapes=[pltpu.SMEM((2 * HALF,), jnp.int32)],
        compiler_params=pltpu.CompilerParams(vmem_limit_bytes=LIMIT),
        name="reorder",
    )(place, destination, pieces, after)


def back_kernel(place_ref, piece_ref, chunk_ref, folded_ref, query_ref, token_ref, attended_ref, arrived_ref, handed_ref):
    row2 = lax.broadcasted_iota(jnp.int32, (2, LANES), 0)
    for tile in range(8):
        columns = slice(tile * LANES, (tile + 1) * LANES)
        lines = []
        for kind in range(2):
            arrived_ref[0, kind, :, columns] = piece_ref[kind * 8 + tile, :BLOCK]
            lines.append(piece_ref[kind * 8 + tile, BLOCK:].astype(jnp.float32))
        for step in range(3):
            both = jnp.where(row2 == 0, lines[0][step : step + 1], lines[1][step : step + 1])
            handed_ref[0, step, :, columns] = both.astype(jnp.bfloat16)

    rank = place_ref[0]
    sources = chunk_ref.shape[0]
    plane = rank // 8
    columns = pl.ds(pl.multiple_of(rank // 2 * LANES, LANES), LANES)
    top = lax.broadcasted_iota(jnp.int32, (8, LANES), 0) < 4
    tables = [chunk_ref[source, plane, 48:CHUNK].astype(jnp.float32) for source in range(sources)]
    tables.append(folded_ref[48:CHUNK].astype(jnp.float32))
    tables.append(jnp.zeros_like(tables[0]))
    tables = jnp.concatenate(tables, axis=0).astype(jnp.bfloat16)
    for pair in range(2):
        fresh_keys, fresh_values = [], []
        for token in range(3):
            a = token_ref[token, 2 * pair, :, columns].astype(jnp.float32)
            b = token_ref[token, 2 * pair + 1, :, columns].astype(jnp.float32)
            fresh_keys.append(jnp.where(top, a[0:1], b[0:1]))
            fresh_values.append(jnp.where(top, a[1:2], b[1:2]))
        for step in range(3):
            own = []
            for r in (2 * pair, 2 * pair + 1):
                wide = query_ref[step, r, pl.ds(pl.multiple_of(rank // 4 * 16, 16), 16), :].astype(jnp.float32)
                own.append(jnp.where(rank // 2 % 2 == 1, wide[8:], wide[:8]))
            a, b = own
            query = jnp.where(
                rank % 2 == 1,
                jnp.where(top, pltpu.roll(a, 4, 0), b),
                jnp.where(top, a, pltpu.roll(b, 4, 0)),
            )
            index = step * 2 + pair
            stats = jnp.dot(tables, spread_of(index), preferred_element_type=jnp.float32)
            peaks = [stats[8 * source : 8 * source + 8, :LANES] for source in range(sources + 1)]
            totals = [stats[8 * source : 8 * source + 8, LANES:] for source in range(sources + 1)]
            parts = [chunk_ref[source, plane, 8 * index : 8 * index + 8] for source in range(sources)]
            parts.append(folded_ref[8 * index : 8 * index + 8])
            scores = [
                jnp.sum(query * fresh_keys[token], axis=1, keepdims=True) * FACTOR for token in range(step + 1)
            ]
            joint = functools.reduce(jnp.maximum, peaks + scores)
            total = jnp.zeros((8, LANES), jnp.float32)
            summed = jnp.zeros((8, LANES), jnp.float32)
            for peak, share, part in zip(peaks, totals, parts, strict=True):
                scale = jnp.exp(peak - joint)
                total += share * scale
                summed += part.astype(jnp.float32) * scale
            for token in range(step + 1):
                weight = jnp.exp(scores[token] - joint)
                total += weight
                summed += weight.astype(jnp.bfloat16).astype(jnp.float32) * fresh_values[token]
            attended = summed / total
            attended_ref[step, 2 * pair] = attended[:4].astype(jnp.bfloat16)
            attended_ref[step, 2 * pair + 1] = attended[4:].astype(jnp.bfloat16)


def back(place, pieces, chunks, folded, queries, new_kv):
    steps, req_dev, _, head_dim = queries.shape
    width = new_kv.shape[-1]
    return pl.pallas_call(
        back_kernel,
        in_specs=[pl.BlockSpec(memory_space=pltpu.SMEM)] + [pl.BlockSpec(memory_space=pltpu.VMEM)] * 5,
        out_specs=[pl.BlockSpec(memory_space=pltpu.VMEM)] * 3,
        out_shape=(
            jax.ShapeDtypeStruct((steps, req_dev, 4, head_dim), jnp.bfloat16),
            jax.ShapeDtypeStruct((1, 2, BLOCK, width), jnp.bfloat16),
            jax.ShapeDtypeStruct((1, steps, 2, width), jnp.bfloat16),
        ),
        compiler_params=pltpu.CompilerParams(vmem_limit_bytes=LIMIT),
        name="back",
    )(place, pieces, chunks, folded, queries, new_kv)


def body(kv_cache, lengths, queries, new_kv, moving_slot, destination, block_index):
    place = jnp.stack([lax.axis_index("tp"), lax.axis_index("replica"), moving_slot[0], block_index[0]])
    place = place.astype(jnp.int32)
    local = front(place, lengths, kv_cache, queries)
    planes = [list(range(8)), list(range(8, 16))]
    chunks = lax.all_to_all(local, "tp", 0, 0, tiled=True, axis_index_groups=planes)
    sent, half_sum = fold(place, chunks, kv_cache, new_kv)
    folded = lax.ppermute(half_sum, "tp", [(i, i ^ 8) for i in range(16)])
    pieces = lax.all_to_all(sent, "replica", 0, 0, tiled=True)
    ordered = reorder(place, destination, pieces, folded)
    halves = [list(range(HALF)), list(range(HALF, 2 * HALF))]
    delivered = lax.all_to_all(ordered, "replica", 0, 0, tiled=True, axis_index_groups=halves)
    return back(place, delivered, chunks, folded, queries, new_kv)


def solution(mesh):
    placed = (
        P("replica", None, "tp", None),
        P("replica"),
        P(None, "replica", None, None),
        P(None, "replica", None, None),
        P("replica"),
        P(),
        P("replica"),
    )
    return jax.shard_map(
        body,
        mesh=mesh,
        in_specs=placed,
        out_specs=(
            P(None, "replica", "tp", None),
            P("replica", None, "tp", None),
            P("replica", None, None, None),
        ),
        check_vma=False,
    )
```

time: 433 us -> 73.9 us (0.17)
  the two profiles are of different devices: /device:TPU:1 before, /device:TPU:2 now
where the time goes in v2:
time: 73.9 us; the launch traced here: 73.5 us
  blocking collectives  25.2 us (34%)
  starting transfers between devices  23.9 us (32%)
  waiting for transfers between devices  13.1 us (18%)
  Pallas kernels  8.52 us (12%)
  between operations  2.15 us (3%)
    all_to_all x1, starting transfers between devices, body(): pieces = lax.all_to_all(sent, 'replica', 0, 0, tiled=True)  15.7 us
    all_to_all x1, blocking collectives, body(): lax.all_to_all(ordered, 'replica', 0, 0, tiled=True, axis_index_groups=ha...  13.4 us
    all_to_all x1, blocking collectives, body(): lax.all_to_all(local, 'tp', 0, 0, tiled=True, axis_index_groups=planes)  11.8 us
    ppermute x1, starting transfers between devices, body(): folded = lax.ppermute(half_sum, 'tp', [(i, i ^ 8) for i in range(16)])  8.23 us
    all_to_all x1, waiting for transfers between devices, body(): pieces = lax.all_to_all(sent, 'replica', 0, 0, tiled=True)  6.88 us
    ppermute x1, waiting for transfers between devices, body(): folded = lax.ppermute(half_sum, 'tp', [(i, i ^ 8) for i in range(16)])  6.19 us
    pallas_call x1, Pallas kernels, front(): pl.pallas_call(front_kernel, in_specs=[pl.BlockSpec(memory_space=pltpu.SM...  4.77 us
    pallas_call x1, Pallas kernels, fold(): pl.pallas_call(fold_kernel, in_specs=[pl.BlockSpec(memory_space=pltpu.SME...  1.72 us
  transfers between devices with their start and end apart: 2, of which 2 were waited for; matrix products, arithmetic and copies ran while one was open for 0% of the time, Pallas kernels for 0%

profile of v2, /device:TPU:2, one launch (start us, length us, event | category | flops | bytes accessed | tf_op | source)
XLA Modules:
  0.0 73.5 jit_solution(9886091205928688940)
XLA Ops:
  0.6 0.0 copy-start
  0.6 0.0 copy-start.2
  2.1 0.6 pad_add_fusion.place_ref
  2.7 0.0 copy-start.3
  2.7 4.8 %front.1 = bf16[8,2,56,128]{3,2,1,0:T(8,128)(2,1)} custom-call(s32[4]{0:T(128)} %pad_add_fusion.place_ref, s32[4]{0:T(128)} %lengths_hbm.1, bf16[4,2,128,1024]{3,2,1,0:T(8,128)(2,1)} %cache_hbm.3, bf16[3,4,64,128]{3,2,1,0:T(8,128)(2,1)} %query_ref.1), custom_call_target="tpu_custom_call" | custom-call | tf_op jit(solution)/shard_map/front/pallas_call | solution.py:111
  7.5 0.0 copy-start.4
  7.5 0.0 copy-start.1
  7.5 11.8 %all_to_all.15.chunk_ref = bf16[8,2,56,128]{3,2,1,0:T(8,128)(2,1)S(1)} all-to-all(bf16[8,2,56,128]{3,2,1,0:T(8,128)(2,1)} %front.1), channel_id=1, replica_groups={{0,1,2,3,4,5,6,7},{8,9,10,11,12,13,14,15},{16,17,18,19,20,21,22,23},{24..., dimensions={0} | all-to-all | bytes 458752 | tf_op jit(solution)/shard_map/all_to_all | solution.py:324
  19.3 0.0 copy-done
  19.3 0.0 copy-done.2
  19.3 0.0 copy-done.3
  19.3 1.7 %fold.1 = (bf16[32,40,128]{2,1,0:T(8,128)(2,1)}, bf16[56,128]{1,0:T(8,128)(2,1)S(1)}) custom-call(s32[4]{0:T(128)S(1)} %copy-done.3, bf16[8,2,56,128]{3,2,1,0:T(8,128)(2,1)S(1)} %all_to_all.15.chunk_ref, bf16[4,2,128,1024]{3,2,1,0:T(8,128)(2,1)S(1)} %copy-done, bf16[3,4,2,1024]{3,2,1,0:T(2,128)(2,1)S(1)} %copy-done.2), custom_call_target="tpu_custom_call" | custom-call | tf_op jit(solution)/shard_map/fold/pallas_call | solution.py:192
  21.0 15.7 %all-to-all-start.1 = ((bf16[32,40,128]{2,1,0:T(8,128)(2,1)}), bf16[32,40,128]{2,1,0:T(8,128)(2,1)S(1)}, u32[]{:S(2)}, u32[]{:S(2)}) async-start(bf16[32,40,128]{2,1,0:T(8,128)(2,1)} %get-tuple-element.5), calls=%async_computation.1 | async-start | bytes 655360 | tf_op jit(solution)/shard_map/all_to_all | solution.py:327
  36.7 8.2 %collective-permute-start = (bf16[56,128]{1,0:T(8,128)(2,1)S(1)}, bf16[56,128]{1,0:T(8,128)(2,1)S(1)}, u32[]{:S(2)}, u32[]{:S(2)}) collective-permute-start(bf16[56,128]{1,0:T(8,128)(2,1)S(1)} %get-tuple-element.6), channel_id=1, source_target_pairs={{0,8},{1,9},{2,10},{3,11},{4,12},{5,13},{6,14},{7,15},{8,0},{9,1},... | collective-permute-start | bytes 43016 | tf_op jit(solution)/shard_map/ppermute | solution.py:326
  44.9 6.2 %collective-permute-done.after_ref.folded_ref = bf16[56,128]{1,0:T(8,128)(2,1)S(1)} collective-permute-done((bf16[56,128]{1,0:T(8,128)(2,1)S(1)}, bf16[56,128]{1,0:T(8,128)(2,1)S(1)}, u32[]{:S(2)}, u32[]{:S(2)}) %collective-permute-start) | collective-permute-done | bytes 14368 | tf_op jit(solution)/shard_map/ppermute | solution.py:326
  51.1 6.9 %all-to-all-done.1.in_ref = bf16[32,40,128]{2,1,0:T(8,128)(2,1)S(1)} async-done(((bf16[32,40,128]{2,1,0:T(8,128)(2,1)}), bf16[32,40,128]{2,1,0:T(8,128)(2,1)S(1)}, u32[]{:S(2)}, u32[]{:S(2)}) %all-to-all-start.1) | async-done | bytes 327712 | tf_op jit(solution)/shard_map/all_to_all | solution.py:327
  58.0 0.0 copy-done.4
  58.0 0.6 reorder.1
  58.6 13.4 %all_to_all.16.piece_ref = bf16[16,40,128]{2,1,0:T(8,128)(2,1)S(1)} all-to-all(bf16[16,40,128]{2,1,0:T(8,128)(2,1)S(1)} %reorder.1), channel_id=1, replica_groups={{0,16,32,48,64,80,96,112,128,144,160,176,192,208,224,240},{256,272,288,..., dimensions={0} | all-to-all | bytes 327680 | tf_op jit(solution)/shard_map/all_to_all | solution.py:330
  72.0 0.0 copy-done.1
  72.0 1.4 %back.1 = (bf16[3,4,4,128]{3,2,1,0:T(4,128)(2,1)}, bf16[1,2,32,1024]{3,2,1,0:T(8,128)(2,1)}, bf16[1,3,2,1024]{3,2,1,0:T(2,128)(2,1)}) custom-call(s32[4]{0:T(128)S(1)} %copy-done.3, bf16[16,40,128]{2,1,0:T(8,128)(2,1)S(1)} %all_to_all.16.piece_ref, bf16[8,2,56,128]{3,2,1,0:T(8,128)(2,1)S(1)} %all_to_all.15.chunk_ref, ...), custom_call_target="tpu_custom_call" | custom-call | tf_op jit(solution)/shard_map/back/pallas_call | solution.py:305
Async XLA Ops:
  0.6 18.7 %copy-start = (bf16[4,2,128,1024]{3,2,1,0:T(8,128)(2,1)S(1)}, bf16[4,2,128,1024]{3,2,1,0:T(8,128)(2,1)}, u32[]{:S(2)}) copy-start(bf16[4,2,128,1024]{3,2,1,0:T(8,128)(2,1)} %cache_hbm.3) | copy-start | bytes 6291460
  0.6 18.6 %copy-start.2 = (bf16[3,4,2,1024]{3,2,1,0:T(2,128)(2,1)S(1)}, bf16[3,4,2,1024]{3,2,1,0:T(2,128)(2,1)}, u32[]{:S(2)}) copy-start(bf16[3,4,2,1024]{3,2,1,0:T(2,128)(2,1)} %token_ref.1) | copy-start | bytes 147460
  2.7 16.6 %copy-start.3 = (s32[4]{0:T(128)S(1)}, s32[4]{0:T(128)}, u32[]{:S(2)}) copy-start(s32[4]{0:T(128)} %pad_add_fusion.place_ref) | copy-start | bytes 52
  7.5 50.6 %copy-start.4 = (s32[32]{0:T(128)S(1)}, s32[32]{0:T(128)}, u32[]{:S(2)}) copy-start(s32[32]{0:T(128)} %destination_ref.1) | copy-start | bytes 388
  7.5 64.6 %copy-start.1 = (bf16[3,4,64,128]{3,2,1,0:T(8,128)(2,1)S(1)}, bf16[3,4,64,128]{3,2,1,0:T(8,128)(2,1)}, u32[]{:S(2)}) copy-start(bf16[3,4,64,128]{3,2,1,0:T(8,128)(2,1)} %query_ref.1) | copy-start | bytes 589828
  21.0 37.0 %all-to-all-start.1 = ((bf16[32,40,128]{2,1,0:T(8,128)(2,1)}), bf16[32,40,128]{2,1,0:T(8,128)(2,1)S(1)}, u32[]{:S(2)}, u32[]{:S(2)}) async-start(bf16[32,40,128]{2,1,0:T(8,128)(2,1)} %get-tuple-element.5), calls=%async_computation.1 | async-start | bytes 655360 | tf_op jit(solution)/shard_map/all_to_all | solution.py:327
  36.7 14.4 %collective-permute-start = (bf16[56,128]{1,0:T(8,128)(2,1)S(1)}, bf16[56,128]{1,0:T(8,128)(2,1)S(1)}, u32[]{:S(2)}, u32[]{:S(2)}) collective-permute-start(bf16[56,128]{1,0:T(8,128)(2,1)S(1)} %get-tuple-element.6), channel_id=1, source_target_pairs={{0,8},{1,9},{2,10},{3,11},{4,12},{5,13},{6,14},{7,15},{8,0},{9,1},... | collective-permute-start | bytes 43016 | tf_op jit(solution)/shard_map/ppermute | solution.py:326

commit v3 on v2

--- a/solution.py
+++ b/solution.py
@@ -19,10 +19,54 @@
 FRONT_LIMIT = 61 << 20
 
 
+def pack_kernel(slot_ref, block_ref, cache_hbm, token_hbm, sent_ref, moving_ref, token_ref, moving_sem, token_sem):
+    slot = slot_ref[0]
+    first = pl.multiple_of(block_ref[0] * BLOCK, BLOCK)
+    moving_copy = pltpu.make_async_copy(cache_hbm.at[slot, :, pl.ds(first, BLOCK)], moving_ref, moving_sem)
+    moving_copy.start()
+    token_copy = pltpu.make_async_copy(token_hbm, token_ref, token_sem)
+    token_copy.start()
+    row = lax.broadcasted_iota(jnp.int32, (8, LANES), 0)
+    token_copy.wait()
+    lines = [token_ref[step, slot].astype(jnp.float32) for step in range(3)]
+    moving_copy.wait()
+    for kind in range(2):
+        for tile in range(8):
+            columns = slice(tile * LANES, (tile + 1) * LANES)
+            tokens = jnp.zeros((8, LANES), jnp.float32)
+            for step in range(3):
+                tokens = jnp.where(row == step, lines[step][kind : kind + 1, columns], tokens)
+            sent_ref[kind * 8 + tile, :BLOCK] = moving_ref[kind, :, columns]
+            sent_ref[kind * 8 + tile, BLOCK:] = tokens.astype(jnp.bfloat16)
+
+
+def pack(moving_slot, block_index, kv_cache, new_kv):
+    return pl.pallas_call(
+        pack_kernel,
+        in_specs=[
+            pl.BlockSpec(memory_space=pltpu.SMEM),
+            pl.BlockSpec(memory_space=pltpu.SMEM),
+            pl.BlockSpec(memory_space=pl.ANY),
+            pl.BlockSpec(memory_space=pl.ANY),
+        ],
+        out_specs=pl.BlockSpec(memory_space=pltpu.VMEM),
+        out_shape=jax.ShapeDtypeStruct((HALF, SLOT, LANES), jnp.bfloat16),
+        scratch_shapes=[
+            pltpu.VMEM((2, BLOCK, kv_cache.shape[-1]), jnp.bfloat16),
+            pltpu.VMEM(new_kv.shape, jnp.bfloat16),
+            pltpu.SemaphoreType.DMA(()),
+            pltpu.SemaphoreType.DMA(()),
+        ],
+        compiler_params=pltpu.CompilerParams(vmem_limit_bytes=FRONT_LIMIT),
+        name="pack",
+    )(moving_slot, block_index, kv_cache, new_kv)
+
+
 def front_kernel(
-    place_ref, lengths_hbm, cache_hbm, query_hbm, local_ref,
+    lengths_hbm, cache_hbm, query_hbm, after_ref, local_ref,
     lengths_ref, cache_ref, query_ref, lengths_sem, cache_sem, query_sem,
 ):
+    del after_ref
     requests, _, pos_dev, _ = cache_ref.shape
     lengths_copy = pltpu.make_async_copy(lengths_hbm, lengths_ref, lengths_sem)
     lengths_copy.start()
@@ -34,7 +78,7 @@
     for copy in cache_copies:
         copy.start()
 
-    position = place_ref[0] * pos_dev + lax.broadcasted_iota(jnp.int32, (8, pos_dev), 1)
+    position = lax.axis_index("tp") * pos_dev + lax.broadcasted_iota(jnp.int32, (8, pos_dev), 1)
     lane = lax.broadcasted_iota(jnp.int32, (8, LANES), 1)
     top = lax.broadcasted_iota(jnp.int32, (8, LANES), 0) < 4
     lengths_copy.wait()
@@ -106,11 +150,11 @@
                 local_ref[here] = table.astype(jnp.bfloat16)
 
 
-def front(place, lengths, kv_cache, queries):
+def front(lengths, kv_cache, queries, after):
     req_dev = kv_cache.shape[0]
     return pl.pallas_call(
         front_kernel,
-        in_specs=[pl.BlockSpec(memory_space=pltpu.SMEM)] + [pl.BlockSpec(memory_space=pl.ANY)] * 3,
+        in_specs=[pl.BlockSpec(memory_space=pl.ANY)] * 4,
         out_specs=pl.BlockSpec(memory_space=pltpu.VMEM),
         out_shape=jax.ShapeDtypeStruct((8, 2, CHUNK, LANES), jnp.bfloat16),
         scratch_shapes=[
@@ -123,7 +167,7 @@
         ],
         compiler_params=pltpu.CompilerParams(vmem_limit_bytes=FRONT_LIMIT),
         name="front",
-    )(place, lengths, kv_cache, queries)
+    )(lengths, kv_cache, queries, after)
 
 
 def spread_of(index):
@@ -134,16 +178,12 @@
     return jnp.where(second, totals, maxima).astype(jnp.bfloat16)
 
 
-def fold_kernel(
-    place_ref, chunk_ref, cache_hbm, token_hbm, sent_ref, out_ref, moving_ref, token_ref, moving_sem, token_sem
-):
-    slot = place_ref[2]
-    first = pl.multiple_of(place_ref[3] * BLOCK, BLOCK)
-    moving_copy = pltpu.make_async_copy(cache_hbm.at[slot, :, pl.ds(first, BLOCK)], moving_ref, moving_sem)
-    moving_copy.start()
-    token_copy = pltpu.make_async_copy(token_hbm, token_ref, token_sem)
-    token_copy.start()
-    other = 1 - place_ref[0] // 8
+def fold_kernel(destination_ref, chunk_ref, piece_ref, slot_ref, out_ref, source_ref):
+    for source in range(2 * HALF):
+        source_ref[destination_ref[source]] = source
+    for target in range(2 * HALF):
+        slot_ref[target] = piece_ref[source_ref[target] % HALF]
+    other = 1 - lax.axis_index("tp") // 8
     sources = chunk_ref.shape[0]
     lane = lax.broadcasted_iota(jnp.int32, (8, LANES), 1)
     tables = jnp.concatenate(
@@ -172,82 +212,55 @@
             joined = jnp.where(lane == index * 8 + term, value, joined)
     out_ref[48:CHUNK] = joined.astype(jnp.bfloat16)
 
-    token_copy.wait()
-    moving_copy.wait()
-    row = lax.broadcasted_iota(jnp.int32, (8, LANES), 0)
-    lines = [token_ref[step, slot].astype(jnp.float32) for step in range(3)]
-    for kind in range(2):
-        for tile in range(8):
-            columns = slice(tile * LANES, (tile + 1) * LANES)
-            tokens = jnp.zeros((8, LANES), jnp.float32)
-            for step in range(3):
-                tokens = jnp.where(row == step, lines[step][kind : kind + 1, columns], tokens)
-            piece, tokens = moving_ref[kind, :, columns], tokens.astype(jnp.bfloat16)
-            for half in range(2):
-                sent_ref[half * HALF + kind * 8 + tile, :BLOCK] = piece
-                sent_ref[half * HALF + kind * 8 + tile, BLOCK:] = tokens
-
-
-def fold(place, chunks, kv_cache, new_kv):
+
+def fold(destination, chunks, pieces):
     return pl.pallas_call(
         fold_kernel,
-        in_specs=[
-            pl.BlockSpec(memory_space=pltpu.SMEM),
-            pl.BlockSpec(memory_space=pltpu.VMEM),
-            pl.BlockSpec(memory_space=pl.ANY),
-            pl.BlockSpec(memory_space=pl.ANY),
-        ],
+        in_specs=[pl.BlockSpec(memory_space=pltpu.SMEM)] + [pl.BlockSpec(memory_space=pltpu.VMEM)] * 2,
         out_specs=[pl.BlockSpec(memory_space=pltpu.VMEM)] * 2,
         out_shape=(
             jax.ShapeDtypeStruct((2 * HALF, SLOT, LANES), jnp.bfloat16),
             jax.ShapeDtypeStruct((CHUNK, LANES), jnp.bfloat16),
         ),
-        scratch_shapes=[
-            pltpu.VMEM((2, BLOCK, kv_cache.shape[-1]), jnp.bfloat16),
-            pltpu.VMEM(new_kv.shape, jnp.bfloat16),
-            pltpu.SemaphoreType.DMA(()),
-            pltpu.SemaphoreType.DMA(()),
-        ],
+        scratch_shapes=[pltpu.SMEM((2 * HALF,), jnp.int32)],
         compiler_params=pltpu.CompilerParams(vmem_limit_bytes=LIMIT),
         name="fold",
-    )(place, chunks, kv_cache, new_kv)
-
-
-def reorder_kernel(place_ref, destination_ref, in_ref, after_ref, out_ref, source_ref):
-    del after_ref
+    )(destination, chunks, pieces)
+
+
+def unpack_kernel(destination_ref, piece_ref, arrived_ref, handed_ref):
+    mine = lax.axis_index("replica")
+    origin = jnp.int32(0)
     for source in range(2 * HALF):
-        source_ref[destination_ref[source]] = source
-    base = place_ref[1] // HALF * HALF
-    for slot in range(HALF):
-        out_ref[slot] = in_ref[source_ref[base + slot]]
-
-
-def reorder(place, destination, pieces, after):
-    return pl.pallas_call(
-        reorder_kernel,
-        in_specs=[pl.BlockSpec(memory_space=pltpu.SMEM)] * 2
-        + [pl.BlockSpec(memory_space=pltpu.VMEM), pl.BlockSpec(memory_space=pl.ANY)],
-        out_specs=pl.BlockSpec(memory_space=pltpu.VMEM),
-        out_shape=jax.ShapeDtypeStruct((HALF, SLOT, LANES), jnp.bfloat16),
-        scratch_shapes=[pltpu.SMEM((2 * HALF,), jnp.int32)],
-        compiler_params=pltpu.CompilerParams(vmem_limit_bytes=LIMIT),
-        name="reorder",
-    )(place, destination, pieces, after)
-
-
-def back_kernel(place_ref, piece_ref, chunk_ref, folded_ref, query_ref, token_ref, attended_ref, arrived_ref, handed_ref):
-    row2 = lax.broadcasted_iota(jnp.int32, (2, LANES), 0)
+        origin = jnp.where(destination_ref[source] == mine, source // HALF * HALF, origin)
+    row = lax.broadcasted_iota(jnp.int32, (2, LANES), 0)
     for tile in range(8):
         columns = slice(tile * LANES, (tile + 1) * LANES)
         lines = []
         for kind in range(2):
-            arrived_ref[0, kind, :, columns] = piece_ref[kind * 8 + tile, :BLOCK]
-            lines.append(piece_ref[kind * 8 + tile, BLOCK:].astype(jnp.float32))
+            arrived_ref[0, kind, :, columns] = piece_ref[origin + kind * 8 + tile, :BLOCK]
+            lines.append(piece_ref[origin + kind * 8 + tile, BLOCK:].astype(jnp.float32))
         for step in range(3):
-            both = jnp.where(row2 == 0, lines[0][step : step + 1], lines[1][step : step + 1])
+            both = jnp.where(row == 0, lines[0][step : step + 1], lines[1][step : step + 1])
             handed_ref[0, step, :, columns] = both.astype(jnp.bfloat16)
 
-    rank = place_ref[0]
+
+def unpack(destination, pieces, width):
+    return pl.pallas_call(
+        unpack_kernel,
+        in_specs=[pl.BlockSpec(memory_space=pltpu.SMEM), pl.BlockSpec(memory_space=pltpu.VMEM)],
+        out_specs=[pl.BlockSpec(memory_space=pltpu.VMEM)] * 2,
+        out_shape=(
+            jax.ShapeDtypeStruct((1, 2, BLOCK, width), jnp.bfloat16),
+            jax.ShapeDtypeStruct((1, 3, 2, width), jnp.bfloat16),
+        ),
+        compiler_params=pltpu.CompilerParams(vmem_limit_bytes=LIMIT),
+        name="unpack",
+    )(destination, pieces)
+
+
+def merge_kernel(chunk_ref, folded_ref, query_ref, token_ref, attended_ref):
+    rank = lax.axis_index("tp")
     sources = chunk_ref.shape[0]
     plane = rank // 8
     columns = pl.ds(pl.multiple_of(rank // 2 * LANES, LANES), LANES)
@@ -299,36 +312,32 @@
             attended_ref[step, 2 * pair + 1] = attended[4:].astype(jnp.bfloat16)
 
 
-def back(place, pieces, chunks, folded, queries, new_kv):
+def merge(chunks, folded, queries, new_kv):
     steps, req_dev, _, head_dim = queries.shape
-    width = new_kv.shape[-1]
-    return pl.pallas_call(
-        back_kernel,
-        in_specs=[pl.BlockSpec(memory_space=pltpu.SMEM)] + [pl.BlockSpec(memory_space=pltpu.VMEM)] * 5,
-        out_specs=[pl.BlockSpec(memory_space=pltpu.VMEM)] * 3,
-        out_shape=(
-            jax.ShapeDtypeStruct((steps, req_dev, 4, head_dim), jnp.bfloat16),
-            jax.ShapeDtypeStruct((1, 2, BLOCK, width), jnp.bfloat16),
-            jax.ShapeDtypeStruct((1, steps, 2, width), jnp.bfloat16),
-        ),
+    return pl.pallas_call(
+        merge_kernel,
+        in_specs=[pl.BlockSpec(memory_space=pltpu.VMEM)] * 4,
+        out_specs=pl.BlockSpec(memory_space=pltpu.VMEM),
+        out_shape=jax.ShapeDtypeStruct((steps, req_dev, 4, head_dim), jnp.bfloat16),
         compiler_params=pltpu.CompilerParams(vmem_limit_bytes=LIMIT),
-        name="back",
-    )(place, pieces, chunks, folded, queries, new_kv)
+        name="merge",
+    )(chunks, folded, queries, new_kv)
 
 
 def body(kv_cache, lengths, queries, new_kv, moving_slot, destination, block_index):
-    place = jnp.stack([lax.axis_index("tp"), lax.axis_index("replica"), moving_slot[0], block_index[0]])
-    place = place.astype(jnp.int32)
-    local = front(place, lengths, kv_cache, queries)
+    halves = [list(range(HALF)), list(range(HALF, 2 * HALF))]
     planes = [list(range(8)), list(range(8, 16))]
+    packed = pack(moving_slot, block_index, kv_cache, new_kv)
+    pieces = lax.all_to_all(packed, "replica", 0, 0, tiled=True, axis_index_groups=halves)
+    local = front(lengths, kv_cache, queries, packed)
+    local, pieces = lax.optimization_barrier((local, pieces))
     chunks = lax.all_to_all(local, "tp", 0, 0, tiled=True, axis_index_groups=planes)
-    sent, half_sum = fold(place, chunks, kv_cache, new_kv)
+    ordered, half_sum = fold(destination, chunks, pieces)
     folded = lax.ppermute(half_sum, "tp", [(i, i ^ 8) for i in range(16)])
-    pieces = lax.all_to_all(sent, "replica", 0, 0, tiled=True)
-    ordered = reorder(place, destination, pieces, folded)
-    halves = [list(range(HALF)), list(range(HALF, 2 * HALF))]
-    delivered = lax.all_to_all(ordered, "replica", 0, 0, tiled=True, axis_index_groups=halves)
-    return back(place, delivered, chunks, folded, queries, new_kv)
+    delivered = lax.all_to_all(ordered, "replica", 0, 0, tiled=True)
+    attended = merge(chunks, folded, queries, new_kv)
+    arrived, handed = unpack(destination, delivered, kv_cache.shape[-1])
+    return (attended, arrived, handed)
 
 
 def solution(mesh):

time: 73.9 us -> 67.9 us (0.919)
  blocking collectives: 25.2 us -> 11.3 us
  starting transfers between devices: 23.9 us -> 28.8 us
  waiting for transfers between devices: 13.1 us -> 16 us
  Pallas kernels: 8.52 us -> 9.32 us
    all_to_all x1 -> x0, blocking collectives: 13.4 us -> none  [body(): lax.all_to_all(ordered, 'replica', 0, 0, tiled=True, axis_index_groups=ha...]
    all_to_all x1 -> x2, starting transfers between devices: 15.7 us -> 20.6 us  [the longest x1 11.3 us: body(): delivered = lax.all_to_all(ordered, 'replica', 0, 0, tiled=True)]
    all_to_all x1 -> x2, waiting for transfers between devices: 6.88 us -> 9.84 us  [the longest x1 6.01 us: body(): delivered = lax.all_to_all(ordered, 'replica', 0, 0, tiled=True)]
    pallas_call x3 -> x4, Pallas kernels: 6.8 us -> 7.79 us  [the longest x1 4.06 us: front(): pl.pallas_call(front_kernel, in_specs=[pl.BlockSpec(memory_space=pl.ANY)]...]
  transfers between devices with their start and end apart: 2 -> 3, of which waited for: 2 -> 3; matrix products, arithmetic and copies ran while one was open for 0% -> 0% of each run, Pallas kernels for 0% -> 7%
where the time goes in v3:
time: 67.9 us; the launch traced here: 67.4 us
  starting transfers between devices  28.8 us (42%)
  waiting for transfers between devices  16 us (24%)
  blocking collectives  11.3 us (17%)
  Pallas kernels  9.32 us (14%)
  between operations  1.98 us (3%)
    all_to_all x1, starting transfers between devices, body(): delivered = lax.all_to_all(ordered, 'replica', 0, 0, tiled=True)  11.3 us
    all_to_all x1, blocking collectives, body(): lax.all_to_all(local, 'tp', 0, 0, tiled=True, axis_index_groups=planes)  11.3 us
    all_to_all x1, starting transfers between devices, body(): lax.all_to_all(packed, 'replica', 0, 0, tiled=True, axis_index_groups=hal...  9.22 us
    ppermute x1, starting transfers between devices, body(): folded = lax.ppermute(half_sum, 'tp', [(i, i ^ 8) for i in range(16)])  8.23 us
    ppermute x1, waiting for transfers between devices, body(): folded = lax.ppermute(half_sum, 'tp', [(i, i ^ 8) for i in range(16)])  6.19 us
    all_to_all x1, waiting for transfers between devices, body(): delivered = lax.all_to_all(ordered, 'replica', 0, 0, tiled=True)  6.01 us
    pallas_call x1, Pallas kernels, front(): pl.pallas_call(front_kernel, in_specs=[pl.BlockSpec(memory_space=pl.ANY)]...  4.06 us
    all_to_all x1, waiting for transfers between devices, body(): lax.all_to_all(packed, 'replica', 0, 0, tiled=True, axis_index_groups=hal...  3.83 us
  transfers between devices with their start and end apart: 3, of which 3 were waited for; matrix products, arithmetic and copies ran while one was open for 0% of the time, Pallas kernels for 7%

profile of v3, /device:TPU:2, one launch (start us, length us, event | category | flops | bytes accessed | tf_op | source)
XLA Modules:
  0.0 67.4 jit_solution(150437056258673973)
XLA Ops:
  1.9 1.6 %pack.1.after_ref = bf16[16,40,128]{2,1,0:T(8,128)(2,1)} custom-call(s32[1]{0:T(128)S(6)} %copy.10.slot_ref, s32[1]{0:T(128)S(6)} %copy.11.block_ref, bf16[4,2,128,1024]{3,2,1,0:T(8,128)(2,1)} %cache_hbm.3, bf16[3,4,2,1024]{3,2,1,0:T(2,128)(2,1)} %token_ref.1), custom_call_target="tpu_custom_call" | custom-call | tf_op jit(solution)/shard_map/pack/pallas_call | solution.py:44
  3.5 0.0 copy-start.2
  3.6 9.2 %all-to-all-start = ((bf16[16,40,128]{2,1,0:T(8,128)(2,1)}), bf16[16,40,128]{2,1,0:T(8,128)(2,1)S(1)}, u32[]{:S(2)}, u32[]{:S(2)}) async-start(bf16[16,40,128]{2,1,0:T(8,128)(2,1)} %pack.1.after_ref), calls=%async_computation | async-start | bytes 327680 | tf_op jit(solution)/shard_map/all_to_all | solution.py:331
  12.8 0.0 copy-start
  12.8 0.0 copy-start.1
  12.8 4.1 %front.1 = bf16[8,2,56,128]{3,2,1,0:T(8,128)(2,1)} custom-call(s32[4]{0:T(128)} %lengths_hbm.1, bf16[4,2,128,1024]{3,2,1,0:T(8,128)(2,1)} %cache_hbm.3, bf16[3,4,64,128]{3,2,1,0:T(8,128)(2,1)} %query_ref.1, bf16[16,40,128]{2,1,0:T(8,128)(2,1)} %pack.1.after_ref), custom_call_target="tpu_custom_call" | custom-call | tf_op jit(solution)/shard_map/front/pallas_call | solution.py:155
  16.9 3.8 %all-to-all-done.piece_ref = bf16[16,40,128]{2,1,0:T(8,128)(2,1)S(1)} async-done(((bf16[16,40,128]{2,1,0:T(8,128)(2,1)}), bf16[16,40,128]{2,1,0:T(8,128)(2,1)S(1)}, u32[]{:S(2)}, u32[]{:S(2)}) %all-to-all-start) | async-done | bytes 163872 | tf_op jit(solution)/shard_map/all_to_all | solution.py:331
  20.7 11.3 %all_to_all.15.chunk_ref = bf16[8,2,56,128]{3,2,1,0:T(8,128)(2,1)S(1)} all-to-all(bf16[8,2,56,128]{3,2,1,0:T(8,128)(2,1)} %front.1), channel_id=1, replica_groups={{0,1,2,3,4,5,6,7},{8,9,10,11,12,13,14,15},{16,17,18,19,20,21,22,23},{24..., dimensions={0} | all-to-all | bytes 458752 | tf_op jit(solution)/shard_map/all_to_all | solution.py:334
  32.0 0.0 copy-done.2
  32.0 1.5 %fold.1 = (bf16[32,40,128]{2,1,0:T(8,128)(2,1)}, bf16[56,128]{1,0:T(8,128)(2,1)S(1)}) custom-call(s32[32]{0:T(128)S(1)} %copy-done.2, bf16[8,2,56,128]{3,2,1,0:T(8,128)(2,1)S(1)} %all_to_all.15.chunk_ref, bf16[16,40,128]{2,1,0:T(8,128)(2,1)S(1)} %all-to-all-done.piece_ref), custom_call_target="tpu_custom_call" | custom-call | tf_op jit(solution)/shard_map/fold/pallas_call | solution.py:217
  33.5 11.3 %all-to-all-start.2 = ((bf16[32,40,128]{2,1,0:T(8,128)(2,1)}), bf16[32,40,128]{2,1,0:T(8,128)(2,1)S(1)}, u32[]{:S(2)}, u32[]{:S(2)}) async-start(bf16[32,40,128]{2,1,0:T(8,128)(2,1)} %get-tuple-element.12), calls=%async_computation.2 | async-start | bytes 655360 | tf_op jit(solution)/shard_map/all_to_all | solution.py:337
  44.9 8.2 %collective-permute-start = (bf16[56,128]{1,0:T(8,128)(2,1)S(1)}, bf16[56,128]{1,0:T(8,128)(2,1)S(1)}, u32[]{:S(2)}, u32[]{:S(2)}) collective-permute-start(bf16[56,128]{1,0:T(8,128)(2,1)S(1)} %get-tuple-element.11), channel_id=1, source_target_pairs={{0,8},{1,9},{2,10},{3,11},{4,12},{5,13},{6,14},{7,15},{8,0},{9,1},... | collective-permute-start | bytes 43016 | tf_op jit(solution)/shard_map/ppermute | solution.py:336
  53.1 6.2 %collective-permute-done.folded_ref = bf16[56,128]{1,0:T(8,128)(2,1)S(1)} collective-permute-done((bf16[56,128]{1,0:T(8,128)(2,1)S(1)}, bf16[56,128]{1,0:T(8,128)(2,1)S(1)}, u32[]{:S(2)}, u32[]{:S(2)}) %collective-permute-start) | collective-permute-done | bytes 14368 | tf_op jit(solution)/shard_map/ppermute | solution.py:336
  59.3 0.0 copy-done
  59.3 0.0 copy-done.1
  59.3 0.9 %merge.1 = bf16[3,4,4,128]{3,2,1,0:T(4,128)(2,1)} custom-call(bf16[8,2,56,128]{3,2,1,0:T(8,128)(2,1)S(1)} %all_to_all.15.chunk_ref, bf16[56,128]{1,0:T(8,128)(2,1)S(1)} %collective-permute-done.folded_ref, bf16[3,4,64,128]{3,2,1,0:T(8,128)(2,1)S(1)} %copy-done, bf16[3,4,2,1024]{3,2,1,0:T(2,128)(2,1)S(1)} %copy-done.1), custom_call_target="tpu_custom_call" | custom-call | tf_op jit(solution)/shard_map/merge/pallas_call | solution.py:317
  60.2 6.0 %all-to-all-done.2.piece_ref = bf16[32,40,128]{2,1,0:T(8,128)(2,1)S(1)} async-done(((bf16[32,40,128]{2,1,0:T(8,128)(2,1)}), bf16[32,40,128]{2,1,0:T(8,128)(2,1)S(1)}, u32[]{:S(2)}, u32[]{:S(2)}) %all-to-all-start.2) | async-done | bytes 327712 | tf_op jit(solution)/shard_map/all_to_all | solution.py:337
  66.2 1.3 %unpack.1 = (bf16[1,2,32,1024]{3,2,1,0:T(8,128)(2,1)}, bf16[1,3,2,1024]{3,2,1,0:T(2,128)(2,1)}) custom-call(s32[32]{0:T(128)S(1)} %copy-done.2, bf16[32,40,128]{2,1,0:T(8,128)(2,1)S(1)} %all-to-all-done.2.piece_ref), custom_call_target="tpu_custom_call" | custom-call | tf_op jit(solution)/shard_map/unpack/pallas_call | solution.py:249
Async XLA Ops:
  3.5 28.4 %copy-start.2 = (s32[32]{0:T(128)S(1)}, s32[32]{0:T(128)}, u32[]{:S(2)}) copy-start(s32[32]{0:T(128)} %destination_ref.3) | copy-start | bytes 388
  3.6 17.1 %all-to-all-start = ((bf16[16,40,128]{2,1,0:T(8,128)(2,1)}), bf16[16,40,128]{2,1,0:T(8,128)(2,1)S(1)}, u32[]{:S(2)}, u32[]{:S(2)}) async-start(bf16[16,40,128]{2,1,0:T(8,128)(2,1)} %pack.1.after_ref), calls=%async_computation | async-start | bytes 327680 | tf_op jit(solution)/shard_map/all_to_all | solution.py:331
  12.8 46.5 %copy-start = (bf16[3,4,64,128]{3,2,1,0:T(8,128)(2,1)S(1)}, bf16[3,4,64,128]{3,2,1,0:T(8,128)(2,1)}, u32[]{:S(2)}) copy-start(bf16[3,4,64,128]{3,2,1,0:T(8,128)(2,1)} %query_ref.1) | copy-start | bytes 589828
  12.8 46.5 %copy-start.1 = (bf16[3,4,2,1024]{3,2,1,0:T(2,128)(2,1)S(1)}, bf16[3,4,2,1024]{3,2,1,0:T(2,128)(2,1)}, u32[]{:S(2)}) copy-start(bf16[3,4,2,1024]{3,2,1,0:T(2,128)(2,1)} %token_ref.1) | copy-start | bytes 147460
  33.5 32.7 %all-to-all-start.2 = ((bf16[32,40,128]{2,1,0:T(8,128)(2,1)}), bf16[32,40,128]{2,1,0:T(8,128)(2,1)S(1)}, u32[]{:S(2)}, u32[]{:S(2)}) async-start(bf16[32,40,128]{2,1,0:T(8,128)(2,1)} %get-tuple-element.12), calls=%async_computation.2 | async-start | bytes 655360 | tf_op jit(solution)/shard_map/all_to_all | solution.py:337
  44.9 14.4 %collective-permute-start = (bf16[56,128]{1,0:T(8,128)(2,1)S(1)}, bf16[56,128]{1,0:T(8,128)(2,1)S(1)}, u32[]{:S(2)}, u32[]{:S(2)}) collective-permute-start(bf16[56,128]{1,0:T(8,128)(2,1)S(1)} %get-tuple-element.11), channel_id=1, source_target_pairs={{0,8},{1,9},{2,10},{3,11},{4,12},{5,13},{6,14},{7,15},{8,0},{9,1},... | collective-permute-start | bytes 43016 | tf_op jit(solution)/shard_map/ppermute | solution.py:336

commit v4 on v3

--- a/solution.py
+++ b/solution.py
@@ -14,6 +14,9 @@
 CHUNK = 56
 LANES = 128
 HIDDEN = -1e30
+MEMBERS = (13, 11, 15, 10, 5, 29, 24, 4, 22, 19, 27, 20, 3, 2, 14, 25, 9, 18, 12, 31, 16, 28, 7, 26, 21, 1, 23, 17, 30, 8, 0, 6)
+NEAR = (8, 2, 0, 15, 1, 13, 12, 9, 3, 7, 4, 10, 14, 11, 6, 5)
+PLANE = (6, 7, 2, 4, 0, 3, 1, 5)
 FACTOR = 1.0 / math.sqrt(LANES)
 LIMIT = 16 << 20
 FRONT_LIMIT = 61 << 20
@@ -36,8 +39,8 @@
             tokens = jnp.zeros((8, LANES), jnp.float32)
             for step in range(3):
                 tokens = jnp.where(row == step, lines[step][kind : kind + 1, columns], tokens)
-            sent_ref[kind * 8 + tile, :BLOCK] = moving_ref[kind, :, columns]
-            sent_ref[kind * 8 + tile, BLOCK:] = tokens.astype(jnp.bfloat16)
+            sent_ref[NEAR.index(kind * 8 + tile), :BLOCK] = moving_ref[kind, :, columns]
+            sent_ref[NEAR.index(kind * 8 + tile), BLOCK:] = tokens.astype(jnp.bfloat16)
 
 
 def pack(moving_slot, block_index, kv_cache, new_kv):
@@ -132,9 +135,9 @@
             for step in range(3):
                 a, b = sum_a[8 * step : 8 * step + 8], sum_b[8 * step : 8 * step + 8]
                 rows = slice(16 * step + 8 * pair, 16 * step + 8 * pair + 8)
-                here = (2 * head % 8, head // 4, rows)
+                here = (PLANE.index(2 * head % 8), head // 4, rows)
                 local_ref[here] = jnp.where(top, a, pltpu.roll(b, 4, 0)).astype(jnp.bfloat16)
-                here = (2 * head % 8 + 1, head // 4, rows)
+                here = (PLANE.index(2 * head % 8 + 1), head // 4, rows)
                 local_ref[here] = jnp.where(top, pltpu.roll(a, 4, 0), b).astype(jnp.bfloat16)
                 for term in range(5):
                     here = lane == (step * 2 + pair) * 8 + term
@@ -144,7 +147,7 @@
                 (0, jnp.where(top, table_a, pltpu.roll(table_b, 4, 0))),
                 (1, jnp.where(top, pltpu.roll(table_a, 4, 0), table_b)),
             ):
-                here = (2 * head % 8 + half, head // 4, slice(48, CHUNK))
+                here = (PLANE.index(2 * head % 8 + half), head // 4, slice(48, CHUNK))
                 if pair == 1:
                     table = table + local_ref[here].astype(jnp.float32)
                 local_ref[here] = table.astype(jnp.bfloat16)
@@ -178,11 +181,26 @@
     return jnp.where(second, totals, maxima).astype(jnp.bfloat16)
 
 
-def fold_kernel(destination_ref, chunk_ref, piece_ref, slot_ref, out_ref, source_ref):
+def order_kernel(destination_ref, piece_ref, slot_ref, source_ref):
     for source in range(2 * HALF):
-        source_ref[destination_ref[source]] = source
-    for target in range(2 * HALF):
-        slot_ref[target] = piece_ref[source_ref[target] % HALF]
+        source_ref[destination_ref[source]] = NEAR.index(source % HALF)
+    for slot, target in enumerate(MEMBERS):
+        slot_ref[slot] = piece_ref[source_ref[target]]
+
+
+def order(destination, pieces):
+    return pl.pallas_call(
+        order_kernel,
+        in_specs=[pl.BlockSpec(memory_space=pltpu.SMEM), pl.BlockSpec(memory_space=pltpu.VMEM)],
+        out_specs=pl.BlockSpec(memory_space=pltpu.VMEM),
+        out_shape=jax.ShapeDtypeStruct((2 * HALF, SLOT, LANES), jnp.bfloat16),
+        scratch_shapes=[pltpu.SMEM((2 * HALF,), jnp.int32)],
+        compiler_params=pltpu.CompilerParams(vmem_limit_bytes=LIMIT),
+        name="order",
+    )(destination, pieces)
+
+
+def fold_kernel(chunk_ref, out_ref):
     other = 1 - lax.axis_index("tp") // 8
     sources = chunk_ref.shape[0]
     lane = lax.broadcasted_iota(jnp.int32, (8, LANES), 1)
@@ -213,33 +231,31 @@
     out_ref[48:CHUNK] = joined.astype(jnp.bfloat16)
 
 
-def fold(destination, chunks, pieces):
+def fold(chunks):
     return pl.pallas_call(
         fold_kernel,
-        in_specs=[pl.BlockSpec(memory_space=pltpu.SMEM)] + [pl.BlockSpec(memory_space=pltpu.VMEM)] * 2,
-        out_specs=[pl.BlockSpec(memory_space=pltpu.VMEM)] * 2,
-        out_shape=(
-            jax.ShapeDtypeStruct((2 * HALF, SLOT, LANES), jnp.bfloat16),
-            jax.ShapeDtypeStruct((CHUNK, LANES), jnp.bfloat16),
-        ),
-        scratch_shapes=[pltpu.SMEM((2 * HALF,), jnp.int32)],
+        in_specs=[pl.BlockSpec(memory_space=pltpu.VMEM)],
+        out_specs=pl.BlockSpec(memory_space=pltpu.VMEM),
+        out_shape=jax.ShapeDtypeStruct((CHUNK, LANES), jnp.bfloat16),
         compiler_params=pltpu.CompilerParams(vmem_limit_bytes=LIMIT),
         name="fold",
-    )(destination, chunks, pieces)
+    )(chunks)
 
 
 def unpack_kernel(destination_ref, piece_ref, arrived_ref, handed_ref):
     mine = lax.axis_index("replica")
-    origin = jnp.int32(0)
-    for source in range(2 * HALF):
-        origin = jnp.where(destination_ref[source] == mine, source // HALF * HALF, origin)
+    upper = jnp.bool_(False)
+    for source in range(HALF, 2 * HALF):
+        upper = upper | (destination_ref[source] == mine)
+    places = [MEMBERS.index(member) for member in range(2 * HALF)]
+    places = [jnp.where(upper, places[HALF + piece], places[piece]) for piece in range(HALF)]
     row = lax.broadcasted_iota(jnp.int32, (2, LANES), 0)
     for tile in range(8):
         columns = slice(tile * LANES, (tile + 1) * LANES)
         lines = []
         for kind in range(2):
-            arrived_ref[0, kind, :, columns] = piece_ref[origin + kind * 8 + tile, :BLOCK]
-            lines.append(piece_ref[origin + kind * 8 + tile, BLOCK:].astype(jnp.float32))
+            arrived_ref[0, kind, :, columns] = piece_ref[places[kind * 8 + tile], :BLOCK]
+            lines.append(piece_ref[places[kind * 8 + tile], BLOCK:].astype(jnp.float32))
         for step in range(3):
             both = jnp.where(row == 0, lines[0][step : step + 1], lines[1][step : step + 1])
             handed_ref[0, step, :, columns] = both.astype(jnp.bfloat16)
@@ -325,16 +341,17 @@
 
 
 def body(kv_cache, lengths, queries, new_kv, moving_slot, destination, block_index):
-    halves = [list(range(HALF)), list(range(HALF, 2 * HALF))]
-    planes = [list(range(8)), list(range(8, 16))]
+    halves = [NEAR, [HALF + member for member in NEAR]]
+    planes = [PLANE, [8 + member for member in PLANE]]
     packed = pack(moving_slot, block_index, kv_cache, new_kv)
     pieces = lax.all_to_all(packed, "replica", 0, 0, tiled=True, axis_index_groups=halves)
     local = front(lengths, kv_cache, queries, packed)
     local, pieces = lax.optimization_barrier((local, pieces))
     chunks = lax.all_to_all(local, "tp", 0, 0, tiled=True, axis_index_groups=planes)
-    ordered, half_sum = fold(destination, chunks, pieces)
-    folded = lax.ppermute(half_sum, "tp", [(i, i ^ 8) for i in range(16)])
-    delivered = lax.all_to_all(ordered, "replica", 0, 0, tiled=True)
+    ordered = order(destination, pieces)
+    chunks, ordered = lax.optimization_barrier((chunks, ordered))
+    delivered = lax.all_to_all(ordered, "replica", 0, 0, tiled=True, axis_index_groups=[MEMBERS])
+    folded = lax.ppermute(fold(chunks), "tp", [(i, i ^ 8) for i in range(16)])
     attended = merge(chunks, folded, queries, new_kv)
     arrived, handed = unpack(destination, delivered, kv_cache.shape[-1])
     return (attended, arrived, handed)

time: 67.9 us -> 63.5 us (0.935)
  the two profiles are of different devices: /device:TPU:2 before, /device:TPU:64 now
where the time goes in v4:
time: 63.5 us; the launch traced here: 63.1 us
  starting transfers between devices  31.8 us (50%)
  waiting for transfers between devices  19.8 us (31%)
  Pallas kernels  9.37 us (15%)
  between operations  1.99 us (3%)
    ppermute x1, waiting for transfers between devices, body(): folded = lax.ppermute(fold(chunks), 'tp', [(i, i ^ 8) for i in range(16)])  12 us
    all_to_all x1, starting transfers between devices, body(): lax.all_to_all(ordered, 'replica', 0, 0, tiled=True, axis_index_groups=[M...  10.9 us
    ppermute x1, starting transfers between devices, body(): folded = lax.ppermute(fold(chunks), 'tp', [(i, i ^ 8) for i in range(16)])  8.65 us
    all_to_all x1, starting transfers between devices, body(): lax.all_to_all(packed, 'replica', 0, 0, tiled=True, axis_index_groups=hal...  6.42 us
    all_to_all x1, starting transfers between devices, body(): lax.all_to_all(local, 'tp', 0, 0, tiled=True, axis_index_groups=planes)  5.81 us
    all_to_all x1, waiting for transfers between devices, body(): lax.all_to_all(packed, 'replica', 0, 0, tiled=True, axis_index_groups=hal...  4.08 us
    pallas_call x1, Pallas kernels, front(): pl.pallas_call(front_kernel, in_specs=[pl.BlockSpec(memory_space=pl.ANY)]...  4.06 us
    all_to_all x1, waiting for transfers between devices, body(): lax.all_to_all(local, 'tp', 0, 0, tiled=True, axis_index_groups=planes)  3.79 us
  transfers between devices with their start and end apart: 4, of which 3 were waited for; matrix products, arithmetic and copies ran while one was open for 0% of the time, Pallas kernels for 10%

profile of v4, /device:TPU:64, one launch (start us, length us, event | category | flops | bytes accessed | tf_op | source)
XLA Modules:
  0.0 63.1 jit_solution(4760166435150549388)
XLA Ops:
  1.9 1.6 %pack.1.after_ref = bf16[16,40,128]{2,1,0:T(8,128)(2,1)} custom-call(s32[1]{0:T(128)S(6)} %copy.10.slot_ref, s32[1]{0:T(128)S(6)} %copy.11.block_ref, bf16[4,2,128,1024]{3,2,1,0:T(8,128)(2,1)} %cache_hbm.3, bf16[3,4,2,1024]{3,2,1,0:T(2,128)(2,1)} %token_ref.1), custom_call_target="tpu_custom_call" | custom-call | tf_op jit(solution)/shard_map/pack/pallas_call | solution.py:47
  3.6 0.0 copy-start.2
  3.6 6.4 %all-to-all-start = ((bf16[16,40,128]{2,1,0:T(8,128)(2,1)}), bf16[16,40,128]{2,1,0:T(8,128)(2,1)S(1)}, u32[]{:S(2)}, u32[]{:S(2)}) async-start(bf16[16,40,128]{2,1,0:T(8,128)(2,1)} %pack.1.after_ref), calls=%async_computation | async-start | bytes 327680 | tf_op jit(solution)/shard_map/all_to_all | solution.py:347
  10.0 0.0 copy-start
  10.0 0.0 copy-start.1
  10.0 4.1 %front.1 = bf16[8,2,56,128]{3,2,1,0:T(8,128)(2,1)} custom-call(s32[4]{0:T(128)} %lengths_hbm.1, bf16[4,2,128,1024]{3,2,1,0:T(8,128)(2,1)} %cache_hbm.3, bf16[3,4,64,128]{3,2,1,0:T(8,128)(2,1)} %query_ref.1, bf16[16,40,128]{2,1,0:T(8,128)(2,1)} %pack.1.after_ref), custom_call_target="tpu_custom_call" | custom-call | tf_op jit(solution)/shard_map/front/pallas_call | solution.py:158
  14.1 4.1 %all-to-all-done.piece_ref = bf16[16,40,128]{2,1,0:T(8,128)(2,1)S(1)} async-done(((bf16[16,40,128]{2,1,0:T(8,128)(2,1)}), bf16[16,40,128]{2,1,0:T(8,128)(2,1)S(1)}, u32[]{:S(2)}, u32[]{:S(2)}) %all-to-all-start) | async-done | bytes 163872 | tf_op jit(solution)/shard_map/all_to_all | solution.py:347
  18.2 5.8 %all-to-all-start.1 = ((bf16[8,2,56,128]{3,2,1,0:T(8,128)(2,1)}), bf16[8,2,56,128]{3,2,1,0:T(8,128)(2,1)S(1)}, u32[]{:S(2)}, u32[]{:S(2)}) async-start(bf16[8,2,56,128]{3,2,1,0:T(8,128)(2,1)} %front.1), calls=%async_computation.1 | async-start | bytes 458752 | tf_op jit(solution)/shard_map/all_to_all | solution.py:350
  24.0 0.0 copy-done.2
  24.0 1.3 %order.1 = bf16[32,40,128]{2,1,0:T(8,128)(2,1)} custom-call(s32[32]{0:T(128)S(1)} %copy-done.2, bf16[16,40,128]{2,1,0:T(8,128)(2,1)S(1)} %all-to-all-done.piece_ref), custom_call_target="tpu_custom_call" | custom-call | tf_op jit(solution)/shard_map/order/pallas_call | solution.py:192
  25.3 3.8 %all-to-all-done.1.chunk_ref = bf16[8,2,56,128]{3,2,1,0:T(8,128)(2,1)S(1)} async-done(((bf16[8,2,56,128]{3,2,1,0:T(8,128)(2,1)}), bf16[8,2,56,128]{3,2,1,0:T(8,128)(2,1)S(1)}, u32[]{:S(2)}, u32[]{:S(2)}) %all-to-all-start.1) | async-done | bytes 229408 | tf_op jit(solution)/shard_map/all_to_all | solution.py:350
  29.1 10.9 %all-to-all-start.2 = ((bf16[32,40,128]{2,1,0:T(8,128)(2,1)}), bf16[32,40,128]{2,1,0:T(8,128)(2,1)S(1)}, u32[]{:S(2)}, u32[]{:S(2)}) async-start(bf16[32,40,128]{2,1,0:T(8,128)(2,1)} %order.1), calls=%async_computation.2 | async-start | bytes 655360 | tf_op jit(solution)/shard_map/all_to_all | solution.py:353
  40.1 0.2 fold.1
  40.3 8.7 %collective-permute-start = (bf16[56,128]{1,0:T(8,128)(2,1)S(1)}, bf16[56,128]{1,0:T(8,128)(2,1)S(1)}, u32[]{:S(2)}, u32[]{:S(2)}) collective-permute-start(bf16[56,128]{1,0:T(8,128)(2,1)S(1)} %fold.1), channel_id=1, source_target_pairs={{0,8},{1,9},{2,10},{3,11},{4,12},{5,13},{6,14},{7,15},{8,0},{9,1},... | collective-permute-start | bytes 43016 | tf_op jit(solution)/shard_map/ppermute | solution.py:354
  48.9 12.0 %collective-permute-done.folded_ref = bf16[56,128]{1,0:T(8,128)(2,1)S(1)} collective-permute-done((bf16[56,128]{1,0:T(8,128)(2,1)S(1)}, bf16[56,128]{1,0:T(8,128)(2,1)S(1)}, u32[]{:S(2)}, u32[]{:S(2)}) %collective-permute-start) | collective-permute-done | bytes 14368 | tf_op jit(solution)/shard_map/ppermute | solution.py:354
  60.9 0.0 copy-done
  60.9 0.0 copy-done.1
  60.9 0.9 %merge.1 = bf16[3,4,4,128]{3,2,1,0:T(4,128)(2,1)} custom-call(bf16[8,2,56,128]{3,2,1,0:T(8,128)(2,1)S(1)} %all-to-all-done.1.chunk_ref, bf16[56,128]{1,0:T(8,128)(2,1)S(1)} %collective-permute-done.folded_ref, bf16[3,4,64,128]{3,2,1,0:T(8,128)(2,1)S(1)} %copy-done, bf16[3,4,2,1024]{3,2,1,0:T(2,128)(2,1)S(1)} %copy-done.1), custom_call_target="tpu_custom_call" | custom-call | tf_op jit(solution)/shard_map/merge/pallas_call | solution.py:333
  61.8 0.0 all-to-all-done.2.piece_ref
  61.8 1.3 %unpack.1 = (bf16[1,2,32,1024]{3,2,1,0:T(8,128)(2,1)}, bf16[1,3,2,1024]{3,2,1,0:T(2,128)(2,1)}) custom-call(s32[32]{0:T(128)S(1)} %copy-done.2, bf16[32,40,128]{2,1,0:T(8,128)(2,1)S(1)} %all-to-all-done.2.piece_ref), custom_call_target="tpu_custom_call" | custom-call | tf_op jit(solution)/shard_map/unpack/pallas_call | solution.py:265
Async XLA Ops:
  3.6 20.4 %copy-start.2 = (s32[32]{0:T(128)S(1)}, s32[32]{0:T(128)}, u32[]{:S(2)}) copy-start(s32[32]{0:T(128)} %destination_ref.3) | copy-start | bytes 388
  3.6 14.6 %all-to-all-start = ((bf16[16,40,128]{2,1,0:T(8,128)(2,1)}), bf16[16,40,128]{2,1,0:T(8,128)(2,1)S(1)}, u32[]{:S(2)}, u32[]{:S(2)}) async-start(bf16[16,40,128]{2,1,0:T(8,128)(2,1)} %pack.1.after_ref), calls=%async_computation | async-start | bytes 327680 | tf_op jit(solution)/shard_map/all_to_all | solution.py:347
  10.0 50.9 %copy-start = (bf16[3,4,64,128]{3,2,1,0:T(8,128)(2,1)S(1)}, bf16[3,4,64,128]{3,2,1,0:T(8,128)(2,1)}, u32[]{:S(2)}) copy-start(bf16[3,4,64,128]{3,2,1,0:T(8,128)(2,1)} %query_ref.1) | copy-start | bytes 589828
  10.0 50.9 %copy-start.1 = (bf16[3,4,2,1024]{3,2,1,0:T(2,128)(2,1)S(1)}, bf16[3,4,2,1024]{3,2,1,0:T(2,128)(2,1)}, u32[]{:S(2)}) copy-start(bf16[3,4,2,1024]{3,2,1,0:T(2,128)(2,1)} %token_ref.1) | copy-start | bytes 147460
  18.2 10.9 %all-to-all-start.1 = ((bf16[8,2,56,128]{3,2,1,0:T(8,128)(2,1)}), bf16[8,2,56,128]{3,2,1,0:T(8,128)(2,1)S(1)}, u32[]{:S(2)}, u32[]{:S(2)}) async-start(bf16[8,2,56,128]{3,2,1,0:T(8,128)(2,1)} %front.1), calls=%async_computation.1 | async-start | bytes 458752 | tf_op jit(solution)/shard_map/all_to_all | solution.py:350
  29.1 32.7 %all-to-all-start.2 = ((bf16[32,40,128]{2,1,0:T(8,128)(2,1)}), bf16[32,40,128]{2,1,0:T(8,128)(2,1)S(1)}, u32[]{:S(2)}, u32[]{:S(2)}) async-start(bf16[32,40,128]{2,1,0:T(8,128)(2,1)} %order.1), calls=%async_computation.2 | async-start | bytes 655360 | tf_op jit(solution)/shard_map/all_to_all | solution.py:353
  40.3 20.6 %collective-permute-start = (bf16[56,128]{1,0:T(8,128)(2,1)S(1)}, bf16[56,128]{1,0:T(8,128)(2,1)S(1)}, u32[]{:S(2)}, u32[]{:S(2)}) collective-permute-start(bf16[56,128]{1,0:T(8,128)(2,1)S(1)} %fold.1), channel_id=1, source_target_pairs={{0,8},{1,9},{2,10},{3,11},{4,12},{5,13},{6,14},{7,15},{8,0},{9,1},... | collective-permute-start | bytes 43016 | tf_op jit(solution)/shard_map/ppermute | solution.py:354

commit v5 on v4

--- a/solution.py
+++ b/solution.py
@@ -10,11 +10,11 @@
 
 BLOCK = 32
 HALF = 16
-SLOT = 40
+ROWS = 4
 CHUNK = 56
 LANES = 128
 HIDDEN = -1e30
-MEMBERS = (13, 11, 15, 10, 5, 29, 24, 4, 22, 19, 27, 20, 3, 2, 14, 25, 9, 18, 12, 31, 16, 28, 7, 26, 21, 1, 23, 17, 30, 8, 0, 6)
+MEMBERS = (16, 14, 13, 26, 28, 18, 29, 25, 11, 6, 10, 2, 31, 19, 8, 17, 15, 3, 4, 1, 7, 9, 20, 30, 22, 5, 12, 27, 23, 21, 0, 24)
 NEAR = (8, 2, 0, 15, 1, 13, 12, 9, 3, 7, 4, 10, 14, 11, 6, 5)
 PLANE = (6, 7, 2, 4, 0, 3, 1, 5)
 FACTOR = 1.0 / math.sqrt(LANES)
@@ -29,18 +29,24 @@
     moving_copy.start()
     token_copy = pltpu.make_async_copy(token_hbm, token_ref, token_sem)
     token_copy.start()
-    row = lax.broadcasted_iota(jnp.int32, (8, LANES), 0)
+    width = moving_ref.shape[-1]
+    row = lax.broadcasted_iota(jnp.int32, (ROWS, LANES), 0)
     token_copy.wait()
     lines = [token_ref[step, slot].astype(jnp.float32) for step in range(3)]
+    for piece in range(HALF):
+        kind, tile = piece // 8, piece % 8
+        tokens = jnp.zeros((ROWS, LANES), jnp.float32)
+        for step in range(3):
+            line = lines[step][kind : kind + 1, tile * LANES : (tile + 1) * LANES]
+            tokens = jnp.where(row == step, line, tokens)
+        sent_ref[NEAR.index(piece), :, width:] = tokens.astype(jnp.bfloat16)
     moving_copy.wait()
-    for kind in range(2):
-        for tile in range(8):
-            columns = slice(tile * LANES, (tile + 1) * LANES)
-            tokens = jnp.zeros((8, LANES), jnp.float32)
-            for step in range(3):
-                tokens = jnp.where(row == step, lines[step][kind : kind + 1, columns], tokens)
-            sent_ref[NEAR.index(kind * 8 + tile), :BLOCK] = moving_ref[kind, :, columns]
-            sent_ref[NEAR.index(kind * 8 + tile), BLOCK:] = tokens.astype(jnp.bfloat16)
+    for quarter in range(4):
+        kind, first = quarter // 2, quarter % 2 * 16
+        rows = moving_ref[kind, first : first + 16].astype(jnp.float32)
+        for part in range(4):
+            piece = NEAR.index(quarter * 4 + part)
+            sent_ref[piece, :, :width] = rows[ROWS * part : ROWS * part + ROWS].astype(jnp.bfloat16)
 
 
 def pack(moving_slot, block_index, kv_cache, new_kv):
@@ -53,7 +59,7 @@
             pl.BlockSpec(memory_space=pl.ANY),
         ],
         out_specs=pl.BlockSpec(memory_space=pltpu.VMEM),
-        out_shape=jax.ShapeDtypeStruct((HALF, SLOT, LANES), jnp.bfloat16),
+        out_shape=jax.ShapeDtypeStruct((HALF, ROWS, kv_cache.shape[-1] + LANES), jnp.bfloat16),
         scratch_shapes=[
             pltpu.VMEM((2, BLOCK, kv_cache.shape[-1]), jnp.bfloat16),
             pltpu.VMEM(new_kv.shape, jnp.bfloat16),
@@ -193,7 +199,7 @@
         order_kernel,
         in_specs=[pl.BlockSpec(memory_space=pltpu.SMEM), pl.BlockSpec(memory_space=pltpu.VMEM)],
         out_specs=pl.BlockSpec(memory_space=pltpu.VMEM),
-        out_shape=jax.ShapeDtypeStruct((2 * HALF, SLOT, LANES), jnp.bfloat16),
+        out_shape=jax.ShapeDtypeStruct((2 * HALF, *pieces.shape[1:]), jnp.bfloat16),
         scratch_shapes=[pltpu.SMEM((2 * HALF,), jnp.int32)],
         compiler_params=pltpu.CompilerParams(vmem_limit_bytes=LIMIT),
         name="order",
@@ -249,16 +255,17 @@
         upper = upper | (destination_ref[source] == mine)
     places = [MEMBERS.index(member) for member in range(2 * HALF)]
     places = [jnp.where(upper, places[HALF + piece], places[piece]) for piece in range(HALF)]
+    width = arrived_ref.shape[-1]
+    for quarter in range(4):
+        kind, first = quarter // 2, quarter % 2 * 16
+        parts = [piece_ref[places[quarter * 4 + part], :, :width].astype(jnp.float32) for part in range(4)]
+        arrived_ref[0, kind, first : first + 16] = jnp.concatenate(parts, axis=0).astype(jnp.bfloat16)
     row = lax.broadcasted_iota(jnp.int32, (2, LANES), 0)
     for tile in range(8):
-        columns = slice(tile * LANES, (tile + 1) * LANES)
-        lines = []
-        for kind in range(2):
-            arrived_ref[0, kind, :, columns] = piece_ref[places[kind * 8 + tile], :BLOCK]
-            lines.append(piece_ref[places[kind * 8 + tile], BLOCK:].astype(jnp.float32))
+        lines = [piece_ref[places[kind * 8 + tile], :, width:].astype(jnp.float32) for kind in range(2)]
         for step in range(3):
             both = jnp.where(row == 0, lines[0][step : step + 1], lines[1][step : step + 1])
-            handed_ref[0, step, :, columns] = both.astype(jnp.bfloat16)
+            handed_ref[0, step, :, tile * LANES : (tile + 1) * LANES] = both.astype(jnp.bfloat16)
 
 
 def unpack(destination, pieces, width):
@@ -275,16 +282,16 @@
     )(destination, pieces)
 
 
-def merge_kernel(chunk_ref, folded_ref, query_ref, token_ref, attended_ref):
+def own_kernel(chunk_ref, query_ref, token_ref, after_ref, peak_ref, total_ref, summed_ref):
+    del after_ref
     rank = lax.axis_index("tp")
     sources = chunk_ref.shape[0]
     plane = rank // 8
     columns = pl.ds(pl.multiple_of(rank // 2 * LANES, LANES), LANES)
     top = lax.broadcasted_iota(jnp.int32, (8, LANES), 0) < 4
-    tables = [chunk_ref[source, plane, 48:CHUNK].astype(jnp.float32) for source in range(sources)]
-    tables.append(folded_ref[48:CHUNK].astype(jnp.float32))
-    tables.append(jnp.zeros_like(tables[0]))
-    tables = jnp.concatenate(tables, axis=0).astype(jnp.bfloat16)
+    tables = jnp.concatenate(
+        [chunk_ref[source, plane, 48:CHUNK].astype(jnp.float32) for source in range(sources)], axis=0
+    ).astype(jnp.bfloat16)
     for pair in range(2):
         fresh_keys, fresh_values = [], []
         for token in range(3):
@@ -304,40 +311,65 @@
                 jnp.where(top, a, pltpu.roll(b, 4, 0)),
             )
             index = step * 2 + pair
+            rows = slice(8 * index, 8 * index + 8)
             stats = jnp.dot(tables, spread_of(index), preferred_element_type=jnp.float32)
-            peaks = [stats[8 * source : 8 * source + 8, :LANES] for source in range(sources + 1)]
-            totals = [stats[8 * source : 8 * source + 8, LANES:] for source in range(sources + 1)]
-            parts = [chunk_ref[source, plane, 8 * index : 8 * index + 8] for source in range(sources)]
-            parts.append(folded_ref[8 * index : 8 * index + 8])
+            peaks = [stats[8 * source : 8 * source + 8, :LANES] for source in range(sources)]
+            totals = [stats[8 * source : 8 * source + 8, LANES:] for source in range(sources)]
             scores = [
                 jnp.sum(query * fresh_keys[token], axis=1, keepdims=True) * FACTOR for token in range(step + 1)
             ]
             joint = functools.reduce(jnp.maximum, peaks + scores)
             total = jnp.zeros((8, LANES), jnp.float32)
             summed = jnp.zeros((8, LANES), jnp.float32)
-            for peak, share, part in zip(peaks, totals, parts, strict=True):
-                scale = jnp.exp(peak - joint)
-                total += share * scale
-                summed += part.astype(jnp.float32) * scale
+            for source in range(sources):
+                scale = jnp.exp(peaks[source] - joint)
+                total += totals[source] * scale
+                summed += chunk_ref[source, plane, rows].astype(jnp.float32) * scale
             for token in range(step + 1):
                 weight = jnp.exp(scores[token] - joint)
                 total += weight
                 summed += weight.astype(jnp.bfloat16).astype(jnp.float32) * fresh_values[token]
+            peak_ref[rows], total_ref[rows], summed_ref[rows] = joint, total, summed
+
+
+def own(chunks, queries, new_kv, after):
+    return pl.pallas_call(
+        own_kernel,
+        in_specs=[pl.BlockSpec(memory_space=pltpu.VMEM)] * 3 + [pl.BlockSpec(memory_space=pl.ANY)],
+        out_specs=[pl.BlockSpec(memory_space=pltpu.VMEM)] * 3,
+        out_shape=[jax.ShapeDtypeStruct((48, LANES), jnp.float32)] * 3,
+        compiler_params=pltpu.CompilerParams(vmem_limit_bytes=LIMIT),
+        name="own",
+    )(chunks, queries, new_kv, after)
+
+
+def merge_kernel(peak_ref, total_ref, summed_ref, folded_ref, attended_ref):
+    table = folded_ref[48:CHUNK].astype(jnp.float32)
+    table = jnp.concatenate([table, table], axis=0).astype(jnp.bfloat16)
+    for pair in range(2):
+        for step in range(3):
+            index = step * 2 + pair
+            rows = slice(8 * index, 8 * index + 8)
+            stats = jnp.dot(table, spread_of(index), preferred_element_type=jnp.float32)[:8]
+            peak = stats[:, :LANES]
+            joint = jnp.maximum(peak, peak_ref[rows])
+            near, far = jnp.exp(peak_ref[rows] - joint), jnp.exp(peak - joint)
+            total = total_ref[rows] * near + stats[:, LANES:] * far
+            summed = summed_ref[rows] * near + folded_ref[rows].astype(jnp.float32) * far
             attended = summed / total
             attended_ref[step, 2 * pair] = attended[:4].astype(jnp.bfloat16)
             attended_ref[step, 2 * pair + 1] = attended[4:].astype(jnp.bfloat16)
 
 
-def merge(chunks, folded, queries, new_kv):
-    steps, req_dev, _, head_dim = queries.shape
+def merge(parts, folded, shape):
     return pl.pallas_call(
         merge_kernel,
         in_specs=[pl.BlockSpec(memory_space=pltpu.VMEM)] * 4,
         out_specs=pl.BlockSpec(memory_space=pltpu.VMEM),
-        out_shape=jax.ShapeDtypeStruct((steps, req_dev, 4, head_dim), jnp.bfloat16),
+        out_shape=jax.ShapeDtypeStruct(shape, jnp.bfloat16),
         compiler_params=pltpu.CompilerParams(vmem_limit_bytes=LIMIT),
         name="merge",
-    )(chunks, folded, queries, new_kv)
+    )(*parts, folded)
 
 
 def body(kv_cache, lengths, queries, new_kv, moving_slot, destination, block_index):
@@ -351,9 +383,13 @@
     ordered = order(destination, pieces)
     chunks, ordered = lax.optimization_barrier((chunks, ordered))
     delivered = lax.all_to_all(ordered, "replica", 0, 0, tiled=True, axis_index_groups=[MEMBERS])
-    folded = lax.ppermute(fold(chunks), "tp", [(i, i ^ 8) for i in range(16)])
-    attended = merge(chunks, folded, queries, new_kv)
+    half_sum = fold(chunks)
+    folded = lax.ppermute(half_sum, "tp", [(i, i ^ 8) for i in range(16)])
+    parts = own(chunks, queries, new_kv, half_sum)
     arrived, handed = unpack(destination, delivered, kv_cache.shape[-1])
+    steps, req_dev, _, head_dim = queries.shape
+    folded, arrived, handed = lax.optimization_barrier((folded, arrived, handed))
+    attended = merge(parts, folded, (steps, req_dev, 4, head_dim))
     return (attended, arrived, handed)
 
 

time: 63.5 us -> 61.1 us (0.962)
  waiting for transfers between devices: 19.8 us -> 17.1 us
    ppermute x1, waiting for transfers between devices: 12 us -> 3.52 us  [body(): folded = lax.ppermute(half_sum, 'tp', [(i, i ^ 8) for i in range(16)])]
    all_to_all x1, waiting for transfers between devices: 0.01 us -> 5.78 us  [body(): lax.all_to_all(ordered, 'replica', 0, 0, tiled=True, axis_index_groups=[M...]
    ppermute x1, starting transfers between devices: 8.65 us -> 9.35 us  [body(): folded = lax.ppermute(half_sum, 'tp', [(i, i ^ 8) for i in range(16)])]
  transfers between devices with their start and end apart: 4 -> 4, of which waited for: 3 -> 4; matrix products, arithmetic and copies ran while one was open for 0% -> 0% of each run, Pallas kernels for 10% -> 12%
where the time goes in v5:
time: 61.1 us; the launch traced here: 60.7 us
  starting transfers between devices  32.1 us (53%)
  waiting for transfers between devices  17.1 us (28%)
  Pallas kernels  9.43 us (15%)
  between operations  2.02 us (3%)
    all_to_all x1, starting transfers between devices, body(): lax.all_to_all(ordered, 'replica', 0, 0, tiled=True, axis_index_groups=[M...  10.7 us
    ppermute x1, starting transfers between devices, body(): folded = lax.ppermute(half_sum, 'tp', [(i, i ^ 8) for i in range(16)])  9.35 us
    all_to_all x1, starting transfers between devices, body(): lax.all_to_all(packed, 'replica', 0, 0, tiled=True, axis_index_groups=hal...  6.42 us
    all_to_all x1, waiting for transfers between devices, body(): lax.all_to_all(ordered, 'replica', 0, 0, tiled=True, axis_index_groups=[M...  5.78 us
    all_to_all x1, starting transfers between devices, body(): lax.all_to_all(local, 'tp', 0, 0, tiled=True, axis_index_groups=planes)  5.69 us
    pallas_call x1, Pallas kernels, front(): pl.pallas_call(front_kernel, in_specs=[pl.BlockSpec(memory_space=pl.ANY)]...  4.06 us
    all_to_all x1, waiting for transfers between devices, body(): lax.all_to_all(packed, 'replica', 0, 0, tiled=True, axis_index_groups=hal...  3.97 us
    all_to_all x1, waiting for transfers between devices, body(): lax.all_to_all(local, 'tp', 0, 0, tiled=True, axis_index_groups=planes)  3.81 us
  transfers between devices with their start and end apart: 4, of which 4 were waited for; matrix products, arithmetic and copies ran while one was open for 0% of the time, Pallas kernels for 12%

profile of v5, /device:TPU:64, one launch (start us, length us, event | category | flops | bytes accessed | tf_op | source)
XLA Modules:
  0.0 60.7 jit_solution(8039595716649165188)
XLA Ops:
  1.9 1.6 %pack.1.after_ref = bf16[16,4,1152]{2,1,0:T(4,128)(2,1)} custom-call(s32[1]{0:T(128)S(6)} %copy.10.slot_ref, s32[1]{0:T(128)S(6)} %copy.11.block_ref, bf16[4,2,128,1024]{3,2,1,0:T(8,128)(2,1)} %cache_hbm.3, bf16[3,4,2,1024]{3,2,1,0:T(2,128)(2,1)} %token_ref.1), custom_call_target="tpu_custom_call" | custom-call | tf_op jit(solution)/shard_map/pack/pallas_call | solution.py:53
  3.5 0.0 copy-start.2
  3.5 6.4 %all-to-all-start = ((bf16[16,4,1152]{2,1,0:T(4,128)(2,1)}), bf16[16,4,1152]{2,1,0:T(4,128)(2,1)S(1)}, u32[]{:S(2)}, u32[]{:S(2)}) async-start(bf16[16,4,1152]{2,1,0:T(4,128)(2,1)} %pack.1.after_ref), calls=%async_computation | async-start | bytes 294912 | tf_op jit(solution)/shard_map/all_to_all | solution.py:379
  10.0 0.0 copy-start
  10.0 0.0 copy-start.1
  10.0 4.1 %front.1 = bf16[8,2,56,128]{3,2,1,0:T(8,128)(2,1)} custom-call(s32[4]{0:T(128)} %lengths_hbm.1, bf16[4,2,128,1024]{3,2,1,0:T(8,128)(2,1)} %cache_hbm.3, bf16[3,4,64,128]{3,2,1,0:T(8,128)(2,1)} %query_ref.1, bf16[16,4,1152]{2,1,0:T(4,128)(2,1)} %pack.1.after_ref), custom_call_target="tpu_custom_call" | custom-call | tf_op jit(solution)/shard_map/front/pallas_call | solution.py:164
  14.0 4.0 %all-to-all-done.piece_ref = bf16[16,4,1152]{2,1,0:T(4,128)(2,1)S(1)} async-done(((bf16[16,4,1152]{2,1,0:T(4,128)(2,1)}), bf16[16,4,1152]{2,1,0:T(4,128)(2,1)S(1)}, u32[]{:S(2)}, u32[]{:S(2)}) %all-to-all-start) | async-done | bytes 147488 | tf_op jit(solution)/shard_map/all_to_all | solution.py:379
  18.0 5.7 %all-to-all-start.1 = ((bf16[8,2,56,128]{3,2,1,0:T(8,128)(2,1)}), bf16[8,2,56,128]{3,2,1,0:T(8,128)(2,1)S(1)}, u32[]{:S(2)}, u32[]{:S(2)}) async-start(bf16[8,2,56,128]{3,2,1,0:T(8,128)(2,1)} %front.1), calls=%async_computation.1 | async-start | bytes 458752 | tf_op jit(solution)/shard_map/all_to_all | solution.py:382
  23.7 0.0 copy-done.2
  23.7 1.3 %order.1 = bf16[32,4,1152]{2,1,0:T(4,128)(2,1)} custom-call(s32[32]{0:T(128)S(1)} %copy-done.2, bf16[16,4,1152]{2,1,0:T(4,128)(2,1)S(1)} %all-to-all-done.piece_ref), custom_call_target="tpu_custom_call" | custom-call | tf_op jit(solution)/shard_map/order/pallas_call | solution.py:198
  25.0 3.8 %all-to-all-done.1.chunk_ref = bf16[8,2,56,128]{3,2,1,0:T(8,128)(2,1)S(1)} async-done(((bf16[8,2,56,128]{3,2,1,0:T(8,128)(2,1)}), bf16[8,2,56,128]{3,2,1,0:T(8,128)(2,1)S(1)}, u32[]{:S(2)}, u32[]{:S(2)}) %all-to-all-start.1) | async-done | bytes 229408 | tf_op jit(solution)/shard_map/all_to_all | solution.py:382
  28.8 10.7 %all-to-all-start.2 = ((bf16[32,4,1152]{2,1,0:T(4,128)(2,1)}), bf16[32,4,1152]{2,1,0:T(4,128)(2,1)S(1)}, u32[]{:S(2)}, u32[]{:S(2)}) async-start(bf16[32,4,1152]{2,1,0:T(4,128)(2,1)} %order.1), calls=%async_computation.2 | async-start | bytes 589824 | tf_op jit(solution)/shard_map/all_to_all | solution.py:385
  39.5 0.2 fold.1.after_ref
  39.8 9.3 %collective-permute-start = (bf16[56,128]{1,0:T(8,128)(2,1)S(1)}, bf16[56,128]{1,0:T(8,128)(2,1)S(1)}, u32[]{:S(2)}, u32[]{:S(2)}) collective-permute-start(bf16[56,128]{1,0:T(8,128)(2,1)S(1)} %fold.1.after_ref), channel_id=1, source_target_pairs={{0,8},{1,9},{2,10},{3,11},{4,12},{5,13},{6,14},{7,15},{8,0},{9,1},... | collective-permute-start | bytes 43016 | tf_op jit(solution)/shard_map/ppermute | solution.py:387
  49.1 0.0 copy-done
  49.1 0.0 copy-done.1
  49.1 0.2 own.1
  49.4 5.8 %all-to-all-done.2.piece_ref = bf16[32,4,1152]{2,1,0:T(4,128)(2,1)S(1)} async-done(((bf16[32,4,1152]{2,1,0:T(4,128)(2,1)}), bf16[32,4,1152]{2,1,0:T(4,128)(2,1)S(1)}, u32[]{:S(2)}, u32[]{:S(2)}) %all-to-all-start.2) | async-done | bytes 294944 | tf_op jit(solution)/shard_map/all_to_all | solution.py:385
  55.2 1.3 %unpack.1 = (bf16[1,2,32,1024]{3,2,1,0:T(8,128)(2,1)}, bf16[1,3,2,1024]{3,2,1,0:T(2,128)(2,1)}) custom-call(s32[32]{0:T(128)S(1)} %copy-done.2, bf16[32,4,1152]{2,1,0:T(4,128)(2,1)S(1)} %all-to-all-done.2.piece_ref), custom_call_target="tpu_custom_call" | custom-call | tf_op jit(solution)/shard_map/unpack/pallas_call | solution.py:272
  56.4 3.5 %collective-permute-done.folded_ref = bf16[56,128]{1,0:T(8,128)(2,1)S(1)} collective-permute-done((bf16[56,128]{1,0:T(8,128)(2,1)S(1)}, bf16[56,128]{1,0:T(8,128)(2,1)S(1)}, u32[]{:S(2)}, u32[]{:S(2)}) %collective-permute-start) | collective-permute-done | bytes 14368 | tf_op jit(solution)/shard_map/ppermute | solution.py:387
  59.9 0.8 %merge.1 = bf16[3,4,4,128]{3,2,1,0:T(4,128)(2,1)} custom-call(f32[48,128]{1,0:T(8,128)S(1)} %get-tuple-element.18.peak_ref, f32[48,128]{1,0:T(8,128)S(1)} %get-tuple-element.19.total_ref, f32[48,128]{1,0:T(8,128)S(1)} %get-tuple-element.20.summed_ref, bf16[56,128]{1,0:T(8,128)(2,1)S(1)} %collective-permute-done.folded_ref), custom_call_target="tpu_custom_call" | custom-call | tf_op jit(solution)/shard_map/merge/pallas_call | solution.py:365
Async XLA Ops:
  3.5 20.2 %copy-start.2 = (s32[32]{0:T(128)S(1)}, s32[32]{0:T(128)}, u32[]{:S(2)}) copy-start(s32[32]{0:T(128)} %destination_ref.3) | copy-start | bytes 388
  3.5 14.5 %all-to-all-start = ((bf16[16,4,1152]{2,1,0:T(4,128)(2,1)}), bf16[16,4,1152]{2,1,0:T(4,128)(2,1)S(1)}, u32[]{:S(2)}, u32[]{:S(2)}) async-start(bf16[16,4,1152]{2,1,0:T(4,128)(2,1)} %pack.1.after_ref), calls=%async_computation | async-start | bytes 294912 | tf_op jit(solution)/shard_map/all_to_all | solution.py:379
  10.0 39.2 %copy-start = (bf16[3,4,64,128]{3,2,1,0:T(8,128)(2,1)S(1)}, bf16[3,4,64,128]{3,2,1,0:T(8,128)(2,1)}, u32[]{:S(2)}) copy-start(bf16[3,4,64,128]{3,2,1,0:T(8,128)(2,1)} %query_ref.1) | copy-start | bytes 589828
  10.0 39.2 %copy-start.1 = (bf16[3,4,2,1024]{3,2,1,0:T(2,128)(2,1)S(1)}, bf16[3,4,2,1024]{3,2,1,0:T(2,128)(2,1)}, u32[]{:S(2)}) copy-start(bf16[3,4,2,1024]{3,2,1,0:T(2,128)(2,1)} %token_ref.1) | copy-start | bytes 147460
  18.0 10.8 %all-to-all-start.1 = ((bf16[8,2,56,128]{3,2,1,0:T(8,128)(2,1)}), bf16[8,2,56,128]{3,2,1,0:T(8,128)(2,1)S(1)}, u32[]{:S(2)}, u32[]{:S(2)}) async-start(bf16[8,2,56,128]{3,2,1,0:T(8,128)(2,1)} %front.1), calls=%async_computation.1 | async-start | bytes 458752 | tf_op jit(solution)/shard_map/all_to_all | solution.py:382
  28.8 26.3 %all-to-all-start.2 = ((bf16[32,4,1152]{2,1,0:T(4,128)(2,1)}), bf16[32,4,1152]{2,1,0:T(4,128)(2,1)S(1)}, u32[]{:S(2)}, u32[]{:S(2)}) async-start(bf16[32,4,1152]{2,1,0:T(4,128)(2,1)} %order.1), calls=%async_computation.2 | async-start | bytes 589824 | tf_op jit(solution)/shard_map/all_to_all | solution.py:385
  39.8 20.2 %collective-permute-start = (bf16[56,128]{1,0:T(8,128)(2,1)S(1)}, bf16[56,128]{1,0:T(8,128)(2,1)S(1)}, u32[]{:S(2)}, u32[]{:S(2)}) collective-permute-start(bf16[56,128]{1,0:T(8,128)(2,1)S(1)} %fold.1.after_ref), channel_id=1, source_target_pairs={{0,8},{1,9},{2,10},{3,11},{4,12},{5,13},{6,14},{7,15},{8,0},{9,1},... | collective-permute-start | bytes 43016 | tf_op jit(solution)/shard_map/ppermute | solution.py:387

commit v6 on v5

--- a/solution.py
+++ b/solution.py
@@ -14,7 +14,10 @@
 CHUNK = 56
 LANES = 128
 HIDDEN = -1e30
-MEMBERS = (16, 14, 13, 26, 28, 18, 29, 25, 11, 6, 10, 2, 31, 19, 8, 17, 15, 3, 4, 1, 7, 9, 20, 30, 22, 5, 12, 27, 23, 21, 0, 24)
+MEMBERS = (
+    (16, 14, 13, 26, 28, 18, 29, 25, 11, 6, 10, 2, 31, 19, 8, 17, 15, 3, 4, 1, 7, 9, 20, 30, 22, 5, 12, 27, 23, 21, 0, 24),
+    (12, 3, 9, 28, 11, 5, 4, 6, 0, 27, 31, 14, 23, 18, 30, 1, 10, 16, 29, 21, 2, 17, 20, 8, 22, 15, 13, 7, 19, 26, 25, 24),
+)
 NEAR = (8, 2, 0, 15, 1, 13, 12, 9, 3, 7, 4, 10, 14, 11, 6, 5)
 PLANE = (6, 7, 2, 4, 0, 3, 1, 5)
 FACTOR = 1.0 / math.sqrt(LANES)
@@ -190,8 +193,9 @@
 def order_kernel(destination_ref, piece_ref, slot_ref, source_ref):
     for source in range(2 * HALF):
         source_ref[destination_ref[source]] = NEAR.index(source % HALF)
-    for slot, target in enumerate(MEMBERS):
-        slot_ref[slot] = piece_ref[source_ref[target]]
+    lower = lax.axis_index("tp") < 8
+    for slot, targets in enumerate(zip(*MEMBERS, strict=True)):
+        slot_ref[slot] = piece_ref[source_ref[jnp.where(lower, targets[0], targets[1])]]
 
 
 def order(destination, pieces):
@@ -253,7 +257,10 @@
     upper = jnp.bool_(False)
     for source in range(HALF, 2 * HALF):
         upper = upper | (destination_ref[source] == mine)
-    places = [MEMBERS.index(member) for member in range(2 * HALF)]
+    lower = lax.axis_index("tp") < 8
+    places = [
+        jnp.where(lower, MEMBERS[0].index(member), MEMBERS[1].index(member)) for member in range(2 * HALF)
+    ]
     places = [jnp.where(upper, places[HALF + piece], places[piece]) for piece in range(HALF)]
     width = arrived_ref.shape[-1]
     for quarter in range(4):
@@ -382,7 +389,9 @@
     chunks = lax.all_to_all(local, "tp", 0, 0, tiled=True, axis_index_groups=planes)
     ordered = order(destination, pieces)
     chunks, ordered = lax.optimization_barrier((chunks, ordered))
-    delivered = lax.all_to_all(ordered, "replica", 0, 0, tiled=True, axis_index_groups=[MEMBERS])
+    tp_count = lax.axis_size("tp")
+    groups = [[member * tp_count + t for member in MEMBERS[t // 8]] for t in range(tp_count)]
+    delivered = lax.all_to_all(ordered, ("replica", "tp"), 0, 0, tiled=True, axis_index_groups=groups)
     half_sum = fold(chunks)
     folded = lax.ppermute(half_sum, "tp", [(i, i ^ 8) for i in range(16)])
     parts = own(chunks, queries, new_kv, half_sum)

time: 61.1 us -> 60.2 us (0.985)
    ppermute x1, waiting for transfers between devices: 3.52 us -> 2.53 us  [body(): folded = lax.ppermute(half_sum, 'tp', [(i, i ^ 8) for i in range(16)])]
    all_to_all x1, waiting for transfers between devices: 5.78 us -> 6.44 us  [body(): lax.all_to_all(ordered, ('replica', 'tp'), 0, 0, tiled=True, axis_index_g...]
    ppermute x1, starting transfers between devices: 9.35 us -> 8.68 us  [body(): folded = lax.ppermute(half_sum, 'tp', [(i, i ^ 8) for i in range(16)])]
where the time goes in v6:
time: 60.2 us; the launch traced here: 59.7 us
  starting transfers between devices  31.5 us (52%)
  waiting for transfers between devices  16.7 us (28%)
  Pallas kernels  9.48 us (16%)
  between operations  2.02 us (3%)
    all_to_all x1, starting transfers between devices, body(): lax.all_to_all(ordered, ('replica', 'tp'), 0, 0, tiled=True, axis_index_g...  10.7 us
    ppermute x1, starting transfers between devices, body(): folded = lax.ppermute(half_sum, 'tp', [(i, i ^ 8) for i in range(16)])  8.68 us
    all_to_all x1, waiting for transfers between devices, body(): lax.all_to_all(ordered, ('replica', 'tp'), 0, 0, tiled=True, axis_index_g...  6.44 us
    all_to_all x1, starting transfers between devices, body(): lax.all_to_all(packed, 'replica', 0, 0, tiled=True, axis_index_groups=hal...  6.42 us
    all_to_all x1, starting transfers between devices, body(): lax.all_to_all(local, 'tp', 0, 0, tiled=True, axis_index_groups=planes)  5.69 us
    pallas_call x1, Pallas kernels, front(): pl.pallas_call(front_kernel, in_specs=[pl.BlockSpec(memory_space=pl.ANY)]...  4.06 us
    all_to_all x1, waiting for transfers between devices, body(): lax.all_to_all(packed, 'replica', 0, 0, tiled=True, axis_index_groups=hal...  3.97 us
    all_to_all x1, waiting for transfers between devices, body(): lax.all_to_all(local, 'tp', 0, 0, tiled=True, axis_index_groups=planes)  3.77 us
  transfers between devices with their start and end apart: 4, of which 4 were waited for; matrix products, arithmetic and copies ran while one was open for 0% of the time, Pallas kernels for 12%

profile of v6, /device:TPU:64, one launch (start us, length us, event | category | flops | bytes accessed | tf_op | source)
XLA Modules:
  0.0 59.7 jit_solution(12842030503562243718)
XLA Ops:
  1.9 1.6 %pack.1.after_ref = bf16[16,4,1152]{2,1,0:T(4,128)(2,1)} custom-call(s32[1]{0:T(128)S(6)} %copy.10.slot_ref, s32[1]{0:T(128)S(6)} %copy.11.block_ref, bf16[4,2,128,1024]{3,2,1,0:T(8,128)(2,1)} %cache_hbm.3, bf16[3,4,2,1024]{3,2,1,0:T(2,128)(2,1)} %token_ref.1), custom_call_target="tpu_custom_call" | custom-call | tf_op jit(solution)/shard_map/pack/pallas_call | solution.py:56
  3.5 0.0 copy-start.2
  3.5 6.4 %all-to-all-start = ((bf16[16,4,1152]{2,1,0:T(4,128)(2,1)}), bf16[16,4,1152]{2,1,0:T(4,128)(2,1)S(1)}, u32[]{:S(2)}, u32[]{:S(2)}) async-start(bf16[16,4,1152]{2,1,0:T(4,128)(2,1)} %pack.1.after_ref), calls=%async_computation | async-start | bytes 294912 | tf_op jit(solution)/shard_map/all_to_all | solution.py:386
  10.0 0.0 copy-start
  10.0 0.0 copy-start.1
  10.0 4.1 %front.1 = bf16[8,2,56,128]{3,2,1,0:T(8,128)(2,1)} custom-call(s32[4]{0:T(128)} %lengths_hbm.1, bf16[4,2,128,1024]{3,2,1,0:T(8,128)(2,1)} %cache_hbm.3, bf16[3,4,64,128]{3,2,1,0:T(8,128)(2,1)} %query_ref.1, bf16[16,4,1152]{2,1,0:T(4,128)(2,1)} %pack.1.after_ref), custom_call_target="tpu_custom_call" | custom-call | tf_op jit(solution)/shard_map/front/pallas_call | solution.py:167
  14.0 4.0 %all-to-all-done.piece_ref = bf16[16,4,1152]{2,1,0:T(4,128)(2,1)S(1)} async-done(((bf16[16,4,1152]{2,1,0:T(4,128)(2,1)}), bf16[16,4,1152]{2,1,0:T(4,128)(2,1)S(1)}, u32[]{:S(2)}, u32[]{:S(2)}) %all-to-all-start) | async-done | bytes 147488 | tf_op jit(solution)/shard_map/all_to_all | solution.py:386
  18.0 5.7 %all-to-all-start.1 = ((bf16[8,2,56,128]{3,2,1,0:T(8,128)(2,1)}), bf16[8,2,56,128]{3,2,1,0:T(8,128)(2,1)S(1)}, u32[]{:S(2)}, u32[]{:S(2)}) async-start(bf16[8,2,56,128]{3,2,1,0:T(8,128)(2,1)} %front.1), calls=%async_computation.1 | async-start | bytes 458752 | tf_op jit(solution)/shard_map/all_to_all | solution.py:389
  23.7 0.0 copy-done.2
  23.7 1.4 %order.1 = bf16[32,4,1152]{2,1,0:T(4,128)(2,1)} custom-call(s32[32]{0:T(128)S(1)} %copy-done.2, bf16[16,4,1152]{2,1,0:T(4,128)(2,1)S(1)} %all-to-all-done.piece_ref), custom_call_target="tpu_custom_call" | custom-call | tf_op jit(solution)/shard_map/order/pallas_call | solution.py:202
  25.1 3.8 %all-to-all-done.1.chunk_ref = bf16[8,2,56,128]{3,2,1,0:T(8,128)(2,1)S(1)} async-done(((bf16[8,2,56,128]{3,2,1,0:T(8,128)(2,1)}), bf16[8,2,56,128]{3,2,1,0:T(8,128)(2,1)S(1)}, u32[]{:S(2)}, u32[]{:S(2)}) %all-to-all-start.1) | async-done | bytes 229408 | tf_op jit(solution)/shard_map/all_to_all | solution.py:389
  28.8 10.7 %all-to-all-start.2 = ((bf16[32,4,1152]{2,1,0:T(4,128)(2,1)}), bf16[32,4,1152]{2,1,0:T(4,128)(2,1)S(1)}, u32[]{:S(2)}, u32[]{:S(2)}) async-start(bf16[32,4,1152]{2,1,0:T(4,128)(2,1)} %order.1), calls=%async_computation.2 | async-start | bytes 589824 | tf_op jit(solution)/shard_map/all_to_all | solution.py:394
  39.5 0.2 fold.1.after_ref
  39.8 8.7 %collective-permute-start = (bf16[56,128]{1,0:T(8,128)(2,1)S(1)}, bf16[56,128]{1,0:T(8,128)(2,1)S(1)}, u32[]{:S(2)}, u32[]{:S(2)}) collective-permute-start(bf16[56,128]{1,0:T(8,128)(2,1)S(1)} %fold.1.after_ref), channel_id=1, source_target_pairs={{0,8},{1,9},{2,10},{3,11},{4,12},{5,13},{6,14},{7,15},{8,0},{9,1},... | collective-permute-start | bytes 43016 | tf_op jit(solution)/shard_map/ppermute | solution.py:396
  48.5 0.0 copy-done
  48.5 0.0 copy-done.1
  48.5 0.2 own.1
  48.7 6.4 %all-to-all-done.2.piece_ref = bf16[32,4,1152]{2,1,0:T(4,128)(2,1)S(1)} async-done(((bf16[32,4,1152]{2,1,0:T(4,128)(2,1)}), bf16[32,4,1152]{2,1,0:T(4,128)(2,1)S(1)}, u32[]{:S(2)}, u32[]{:S(2)}) %all-to-all-start.2) | async-done | bytes 294944 | tf_op jit(solution)/shard_map/all_to_all | solution.py:394
  55.2 1.3 %unpack.1 = (bf16[1,2,32,1024]{3,2,1,0:T(8,128)(2,1)}, bf16[1,3,2,1024]{3,2,1,0:T(2,128)(2,1)}) custom-call(s32[32]{0:T(128)S(1)} %copy-done.2, bf16[32,4,1152]{2,1,0:T(4,128)(2,1)S(1)} %all-to-all-done.2.piece_ref), custom_call_target="tpu_custom_call" | custom-call | tf_op jit(solution)/shard_map/unpack/pallas_call | solution.py:279
  56.4 2.5 %collective-permute-done.folded_ref = bf16[56,128]{1,0:T(8,128)(2,1)S(1)} collective-permute-done((bf16[56,128]{1,0:T(8,128)(2,1)S(1)}, bf16[56,128]{1,0:T(8,128)(2,1)S(1)}, u32[]{:S(2)}, u32[]{:S(2)}) %collective-permute-start) | collective-permute-done | bytes 14368 | tf_op jit(solution)/shard_map/ppermute | solution.py:396
  59.0 0.8 %merge.1 = bf16[3,4,4,128]{3,2,1,0:T(4,128)(2,1)} custom-call(f32[48,128]{1,0:T(8,128)S(1)} %get-tuple-element.18.peak_ref, f32[48,128]{1,0:T(8,128)S(1)} %get-tuple-element.19.total_ref, f32[48,128]{1,0:T(8,128)S(1)} %get-tuple-element.20.summed_ref, bf16[56,128]{1,0:T(8,128)(2,1)S(1)} %collective-permute-done.folded_ref), custom_call_target="tpu_custom_call" | custom-call | tf_op jit(solution)/shard_map/merge/pallas_call | solution.py:372
Async XLA Ops:
  3.5 20.2 %copy-start.2 = (s32[32]{0:T(128)S(1)}, s32[32]{0:T(128)}, u32[]{:S(2)}) copy-start(s32[32]{0:T(128)} %destination_ref.3) | copy-start | bytes 388
  3.5 14.5 %all-to-all-start = ((bf16[16,4,1152]{2,1,0:T(4,128)(2,1)}), bf16[16,4,1152]{2,1,0:T(4,128)(2,1)S(1)}, u32[]{:S(2)}, u32[]{:S(2)}) async-start(bf16[16,4,1152]{2,1,0:T(4,128)(2,1)} %pack.1.after_ref), calls=%async_computation | async-start | bytes 294912 | tf_op jit(solution)/shard_map/all_to_all | solution.py:386
  10.0 38.5 %copy-start = (bf16[3,4,64,128]{3,2,1,0:T(8,128)(2,1)S(1)}, bf16[3,4,64,128]{3,2,1,0:T(8,128)(2,1)}, u32[]{:S(2)}) copy-start(bf16[3,4,64,128]{3,2,1,0:T(8,128)(2,1)} %query_ref.1) | copy-start | bytes 589828
  10.0 38.5 %copy-start.1 = (bf16[3,4,2,1024]{3,2,1,0:T(2,128)(2,1)S(1)}, bf16[3,4,2,1024]{3,2,1,0:T(2,128)(2,1)}, u32[]{:S(2)}) copy-start(bf16[3,4,2,1024]{3,2,1,0:T(2,128)(2,1)} %token_ref.1) | copy-start | bytes 147460
  18.0 10.8 %all-to-all-start.1 = ((bf16[8,2,56,128]{3,2,1,0:T(8,128)(2,1)}), bf16[8,2,56,128]{3,2,1,0:T(8,128)(2,1)S(1)}, u32[]{:S(2)}, u32[]{:S(2)}) async-start(bf16[8,2,56,128]{3,2,1,0:T(8,128)(2,1)} %front.1), calls=%async_computation.1 | async-start | bytes 458752 | tf_op jit(solution)/shard_map/all_to_all | solution.py:389
  28.8 26.3 %all-to-all-start.2 = ((bf16[32,4,1152]{2,1,0:T(4,128)(2,1)}), bf16[32,4,1152]{2,1,0:T(4,128)(2,1)S(1)}, u32[]{:S(2)}, u32[]{:S(2)}) async-start(bf16[32,4,1152]{2,1,0:T(4,128)(2,1)} %order.1), calls=%async_computation.2 | async-start | bytes 589824 | tf_op jit(solution)/shard_map/all_to_all | solution.py:394
  39.8 19.2 %collective-permute-start = (bf16[56,128]{1,0:T(8,128)(2,1)S(1)}, bf16[56,128]{1,0:T(8,128)(2,1)S(1)}, u32[]{:S(2)}, u32[]{:S(2)}) collective-permute-start(bf16[56,128]{1,0:T(8,128)(2,1)S(1)} %fold.1.after_ref), channel_id=1, source_target_pairs={{0,8},{1,9},{2,10},{3,11},{4,12},{5,13},{6,14},{7,15},{8,0},{9,1},... | collective-permute-start | bytes 43016 | tf_op jit(solution)/shard_map/ppermute | solution.py:396

commit v7 on v6

--- a/solution.py
+++ b/solution.py
@@ -15,7 +15,7 @@
 LANES = 128
 HIDDEN = -1e30
 MEMBERS = (
-    (16, 14, 13, 26, 28, 18, 29, 25, 11, 6, 10, 2, 31, 19, 8, 17, 15, 3, 4, 1, 7, 9, 20, 30, 22, 5, 12, 27, 23, 21, 0, 24),
+    (16, 25, 18, 31, 29, 20, 0, 4, 10, 7, 14, 17, 22, 28, 15, 12, 13, 27, 1, 24, 6, 19, 8, 9, 21, 23, 5, 26, 11, 30, 2, 3),
     (12, 3, 9, 28, 11, 5, 4, 6, 0, 27, 31, 14, 23, 18, 30, 1, 10, 16, 29, 21, 2, 17, 20, 8, 22, 15, 13, 7, 19, 26, 25, 24),
 )
 NEAR = (8, 2, 0, 15, 1, 13, 12, 9, 3, 7, 4, 10, 14, 11, 6, 5)
@@ -30,12 +30,12 @@
     first = pl.multiple_of(block_ref[0] * BLOCK, BLOCK)
     moving_copy = pltpu.make_async_copy(cache_hbm.at[slot, :, pl.ds(first, BLOCK)], moving_ref, moving_sem)
     moving_copy.start()
-    token_copy = pltpu.make_async_copy(token_hbm, token_ref, token_sem)
+    token_copy = pltpu.make_async_copy(token_hbm.at[:, slot], token_ref, token_sem)
     token_copy.start()
     width = moving_ref.shape[-1]
     row = lax.broadcasted_iota(jnp.int32, (ROWS, LANES), 0)
     token_copy.wait()
-    lines = [token_ref[step, slot].astype(jnp.float32) for step in range(3)]
+    lines = [token_ref[step].astype(jnp.float32) for step in range(3)]
     for piece in range(HALF):
         kind, tile = piece // 8, piece % 8
         tokens = jnp.zeros((ROWS, LANES), jnp.float32)
@@ -65,7 +65,7 @@
         out_shape=jax.ShapeDtypeStruct((HALF, ROWS, kv_cache.shape[-1] + LANES), jnp.bfloat16),
         scratch_shapes=[
             pltpu.VMEM((2, BLOCK, kv_cache.shape[-1]), jnp.bfloat16),
-            pltpu.VMEM(new_kv.shape, jnp.bfloat16),
+            pltpu.VMEM((3, 2, new_kv.shape[-1]), jnp.bfloat16),
             pltpu.SemaphoreType.DMA(()),
             pltpu.SemaphoreType.DMA(()),
         ],

time: 60.2 us -> 60.2 us (level)
  no operation moved by 1% of the time
where the time goes in v7:
time: 60.2 us; the launch traced here: 59.7 us
  starting transfers between devices  31.5 us (52%)
  waiting for transfers between devices  16.7 us (28%)
  Pallas kernels  9.48 us (16%)
  between operations  2.02 us (3%)
    all_to_all x1, starting transfers between devices, body(): lax.all_to_all(ordered, ('replica', 'tp'), 0, 0, tiled=True, axis_index_g...  10.7 us
    ppermute x1, starting transfers between devices, body(): folded = lax.ppermute(half_sum, 'tp', [(i, i ^ 8) for i in range(16)])  8.66 us
    all_to_all x1, starting transfers between devices, body(): lax.all_to_all(packed, 'replica', 0, 0, tiled=True, axis_index_groups=hal...  6.42 us
    all_to_all x1, waiting for transfers between devices, body(): lax.all_to_all(ordered, ('replica', 'tp'), 0, 0, tiled=True, axis_index_g...  6.27 us
    all_to_all x1, starting transfers between devices, body(): lax.all_to_all(local, 'tp', 0, 0, tiled=True, axis_index_groups=planes)  5.69 us
    pallas_call x1, Pallas kernels, front(): pl.pallas_call(front_kernel, in_specs=[pl.BlockSpec(memory_space=pl.ANY)]...  4.06 us
    all_to_all x1, waiting for transfers between devices, body(): lax.all_to_all(packed, 'replica', 0, 0, tiled=True, axis_index_groups=hal...  3.97 us
    all_to_all x1, waiting for transfers between devices, body(): lax.all_to_all(local, 'tp', 0, 0, tiled=True, axis_index_groups=planes)  3.77 us
  transfers between devices with their start and end apart: 4, of which 4 were waited for; matrix products, arithmetic and copies ran while one was open for 0% of the time, Pallas kernels for 12%

profile of v7, /device:TPU:64, one launch (start us, length us, event | category | flops | bytes accessed | tf_op | source)
XLA Modules:
  0.0 59.7 jit_solution(16950030812740017247)
XLA Ops:
  1.9 1.6 %pack.1.after_ref = bf16[16,4,1152]{2,1,0:T(4,128)(2,1)} custom-call(s32[1]{0:T(128)S(6)} %copy.10.slot_ref, s32[1]{0:T(128)S(6)} %copy.11.block_ref, bf16[4,2,128,1024]{3,2,1,0:T(8,128)(2,1)} %cache_hbm.3, bf16[3,4,2,1024]{3,2,1,0:T(2,128)(2,1)} %token_ref.1), custom_call_target="tpu_custom_call" | custom-call | tf_op jit(solution)/shard_map/pack/pallas_call | solution.py:56
  3.5 0.0 copy-start.2
  3.5 6.4 %all-to-all-start = ((bf16[16,4,1152]{2,1,0:T(4,128)(2,1)}), bf16[16,4,1152]{2,1,0:T(4,128)(2,1)S(1)}, u32[]{:S(2)}, u32[]{:S(2)}) async-start(bf16[16,4,1152]{2,1,0:T(4,128)(2,1)} %pack.1.after_ref), calls=%async_computation | async-start | bytes 294912 | tf_op jit(solution)/shard_map/all_to_all | solution.py:386
  10.0 0.0 copy-start
  10.0 0.0 copy-start.1
  10.0 4.1 %front.1 = bf16[8,2,56,128]{3,2,1,0:T(8,128)(2,1)} custom-call(s32[4]{0:T(128)} %lengths_hbm.1, bf16[4,2,128,1024]{3,2,1,0:T(8,128)(2,1)} %cache_hbm.3, bf16[3,4,64,128]{3,2,1,0:T(8,128)(2,1)} %query_ref.1, bf16[16,4,1152]{2,1,0:T(4,128)(2,1)} %pack.1.after_ref), custom_call_target="tpu_custom_call" | custom-call | tf_op jit(solution)/shard_map/front/pallas_call | solution.py:167
  14.0 4.0 %all-to-all-done.piece_ref = bf16[16,4,1152]{2,1,0:T(4,128)(2,1)S(1)} async-done(((bf16[16,4,1152]{2,1,0:T(4,128)(2,1)}), bf16[16,4,1152]{2,1,0:T(4,128)(2,1)S(1)}, u32[]{:S(2)}, u32[]{:S(2)}) %all-to-all-start) | async-done | bytes 147488 | tf_op jit(solution)/shard_map/all_to_all | solution.py:386
  18.0 5.7 %all-to-all-start.1 = ((bf16[8,2,56,128]{3,2,1,0:T(8,128)(2,1)}), bf16[8,2,56,128]{3,2,1,0:T(8,128)(2,1)S(1)}, u32[]{:S(2)}, u32[]{:S(2)}) async-start(bf16[8,2,56,128]{3,2,1,0:T(8,128)(2,1)} %front.1), calls=%async_computation.1 | async-start | bytes 458752 | tf_op jit(solution)/shard_map/all_to_all | solution.py:389
  23.7 0.0 copy-done.2
  23.7 1.4 %order.1 = bf16[32,4,1152]{2,1,0:T(4,128)(2,1)} custom-call(s32[32]{0:T(128)S(1)} %copy-done.2, bf16[16,4,1152]{2,1,0:T(4,128)(2,1)S(1)} %all-to-all-done.piece_ref), custom_call_target="tpu_custom_call" | custom-call | tf_op jit(solution)/shard_map/order/pallas_call | solution.py:202
  25.1 3.8 %all-to-all-done.1.chunk_ref = bf16[8,2,56,128]{3,2,1,0:T(8,128)(2,1)S(1)} async-done(((bf16[8,2,56,128]{3,2,1,0:T(8,128)(2,1)}), bf16[8,2,56,128]{3,2,1,0:T(8,128)(2,1)S(1)}, u32[]{:S(2)}, u32[]{:S(2)}) %all-to-all-start.1) | async-done | bytes 229408 | tf_op jit(solution)/shard_map/all_to_all | solution.py:389
  28.8 10.7 %all-to-all-start.2 = ((bf16[32,4,1152]{2,1,0:T(4,128)(2,1)}), bf16[32,4,1152]{2,1,0:T(4,128)(2,1)S(1)}, u32[]{:S(2)}, u32[]{:S(2)}) async-start(bf16[32,4,1152]{2,1,0:T(4,128)(2,1)} %order.1), calls=%async_computation.2 | async-start | bytes 589824 | tf_op jit(solution)/shard_map/all_to_all | solution.py:394
  39.6 0.2 fold.1.after_ref
  39.8 8.7 %collective-permute-start = (bf16[56,128]{1,0:T(8,128)(2,1)S(1)}, bf16[56,128]{1,0:T(8,128)(2,1)S(1)}, u32[]{:S(2)}, u32[]{:S(2)}) collective-permute-start(bf16[56,128]{1,0:T(8,128)(2,1)S(1)} %fold.1.after_ref), channel_id=1, source_target_pairs={{0,8},{1,9},{2,10},{3,11},{4,12},{5,13},{6,14},{7,15},{8,0},{9,1},... | collective-permute-start | bytes 43016 | tf_op jit(solution)/shard_map/ppermute | solution.py:396
  48.5 0.0 copy-done
  48.5 0.0 copy-done.1
  48.5 0.2 own.1
  48.7 6.3 %all-to-all-done.2.piece_ref = bf16[32,4,1152]{2,1,0:T(4,128)(2,1)S(1)} async-done(((bf16[32,4,1152]{2,1,0:T(4,128)(2,1)}), bf16[32,4,1152]{2,1,0:T(4,128)(2,1)S(1)}, u32[]{:S(2)}, u32[]{:S(2)}) %all-to-all-start.2) | async-done | bytes 294944 | tf_op jit(solution)/shard_map/all_to_all | solution.py:394
  55.0 1.3 %unpack.1 = (bf16[1,2,32,1024]{3,2,1,0:T(8,128)(2,1)}, bf16[1,3,2,1024]{3,2,1,0:T(2,128)(2,1)}) custom-call(s32[32]{0:T(128)S(1)} %copy-done.2, bf16[32,4,1152]{2,1,0:T(4,128)(2,1)S(1)} %all-to-all-done.2.piece_ref), custom_call_target="tpu_custom_call" | custom-call | tf_op jit(solution)/shard_map/unpack/pallas_call | solution.py:279
  56.3 2.7 %collective-permute-done.folded_ref = bf16[56,128]{1,0:T(8,128)(2,1)S(1)} collective-permute-done((bf16[56,128]{1,0:T(8,128)(2,1)S(1)}, bf16[56,128]{1,0:T(8,128)(2,1)S(1)}, u32[]{:S(2)}, u32[]{:S(2)}) %collective-permute-start) | collective-permute-done | bytes 14368 | tf_op jit(solution)/shard_map/ppermute | solution.py:396
  59.0 0.8 %merge.1 = bf16[3,4,4,128]{3,2,1,0:T(4,128)(2,1)} custom-call(f32[48,128]{1,0:T(8,128)S(1)} %get-tuple-element.18.peak_ref, f32[48,128]{1,0:T(8,128)S(1)} %get-tuple-element.19.total_ref, f32[48,128]{1,0:T(8,128)S(1)} %get-tuple-element.20.summed_ref, bf16[56,128]{1,0:T(8,128)(2,1)S(1)} %collective-permute-done.folded_ref), custom_call_target="tpu_custom_call" | custom-call | tf_op jit(solution)/shard_map/merge/pallas_call | solution.py:372
Async XLA Ops:
  3.5 20.2 %copy-start.2 = (s32[32]{0:T(128)S(1)}, s32[32]{0:T(128)}, u32[]{:S(2)}) copy-start(s32[32]{0:T(128)} %destination_ref.3) | copy-start | bytes 388
  3.5 14.5 %all-to-all-start = ((bf16[16,4,1152]{2,1,0:T(4,128)(2,1)}), bf16[16,4,1152]{2,1,0:T(4,128)(2,1)S(1)}, u32[]{:S(2)}, u32[]{:S(2)}) async-start(bf16[16,4,1152]{2,1,0:T(4,128)(2,1)} %pack.1.after_ref), calls=%async_computation | async-start | bytes 294912 | tf_op jit(solution)/shard_map/all_to_all | solution.py:386
  10.0 38.5 %copy-start = (bf16[3,4,64,128]{3,2,1,0:T(8,128)(2,1)S(1)}, bf16[3,4,64,128]{3,2,1,0:T(8,128)(2,1)}, u32[]{:S(2)}) copy-start(bf16[3,4,64,128]{3,2,1,0:T(8,128)(2,1)} %query_ref.1) | copy-start | bytes 589828
  10.0 38.5 %copy-start.1 = (bf16[3,4,2,1024]{3,2,1,0:T(2,128)(2,1)S(1)}, bf16[3,4,2,1024]{3,2,1,0:T(2,128)(2,1)}, u32[]{:S(2)}) copy-start(bf16[3,4,2,1024]{3,2,1,0:T(2,128)(2,1)} %token_ref.1) | copy-start | bytes 147460
  18.0 10.8 %all-to-all-start.1 = ((bf16[8,2,56,128]{3,2,1,0:T(8,128)(2,1)}), bf16[8,2,56,128]{3,2,1,0:T(8,128)(2,1)S(1)}, u32[]{:S(2)}, u32[]{:S(2)}) async-start(bf16[8,2,56,128]{3,2,1,0:T(8,128)(2,1)} %front.1), calls=%async_computation.1 | async-start | bytes 458752 | tf_op jit(solution)/shard_map/all_to_all | solution.py:389
  28.8 26.2 %all-to-all-start.2 = ((bf16[32,4,1152]{2,1,0:T(4,128)(2,1)}), bf16[32,4,1152]{2,1,0:T(4,128)(2,1)S(1)}, u32[]{:S(2)}, u32[]{:S(2)}) async-start(bf16[32,4,1152]{2,1,0:T(4,128)(2,1)} %order.1), calls=%async_computation.2 | async-start | bytes 589824 | tf_op jit(solution)/shard_map/all_to_all | solution.py:394
  39.8 19.2 %collective-permute-start = (bf16[56,128]{1,0:T(8,128)(2,1)S(1)}, bf16[56,128]{1,0:T(8,128)(2,1)S(1)}, u32[]{:S(2)}, u32[]{:S(2)}) collective-permute-start(bf16[56,128]{1,0:T(8,128)(2,1)S(1)} %fold.1.after_ref), channel_id=1, source_target_pairs={{0,8},{1,9},{2,10},{3,11},{4,12},{5,13},{6,14},{7,15},{8,0},{9,1},... | collective-permute-start | bytes 43016 | tf_op jit(solution)/shard_map/ppermute | solution.py:396
